TPU v7x, 256 devices: a whole 4x4x8 slice. The times are simulated.
256 devices in a mesh: scan: 8 (over x, y_hi), tile: 32 (over y_lo, z, core).
Axes of the slice: x: 4, y: 4 (y_hi: 2, y_lo: 2; y = y_hi * 2 + y_lo), z: 8, core: 2. Of those that a mesh axis runs over, the one named last changes fastest.
Arguments:
- object_field: float32 [2, 8192, 512], P(None, 'tile'), may hold values from -6 to 6
- probe: float32 [2, 256, 256], replicated, may hold values from -18 to 18
- amplitudes: bfloat16 [8, 32, 12, 256, 256], P('scan', 'tile'), may hold values from 0 to 6
- positions: int32 [8, 32, 12, 2], P('scan', 'tile'), may hold values from 0 to 7936, as said below
- counts: int32 [8, 32], P('scan', 'tile'), may hold values from 1 to 12, as said below
Outputs:
- new_object: float32 [2, 8192, 512], P(None, 'tile')
- new_probe: float32 [2, 256, 256], replicated
- probe_gradient: float32 [2, 256, 256], replicated
Inputs may be any that keep to these rules, and one draw needn't show every extreme that they name: `positions`: every slot of the device at tile t names a window whose first row lies in rows t * 256 to (t + 1) * 256 - 1 and is at most 7936, and whose first column is at most 256; both ends are reached. `counts`: slots at and beyond a device's count are ignored; some device has exactly 12 live slots.
All inputs are finite; a program needn't handle non-finite values.
Results may differ from a plain program's by a relative error of at most 0.0065.
Values may be sent and summed in bfloat16 or wider, within the bound.
No kernel may reach another device: no remote copies, remote signals or barrier semaphores. Data moves between devices by JAX's collectives and lax.ppermute only.
A program may use at most 64 MiB of HBM per device.

v0:
```python
import functools
import math

import jax
import jax.numpy as jnp
import numpy as np
from jax import lax
from jax.experimental import pallas as pl
from jax.experimental.pallas import tpu as pltpu
from jax.sharding import PartitionSpec as P

ITERS = 2
PS = 256
TH = 256
OW = 512
CAP = 12
NS = 8
NT = 32
SR = TH // NS
LN = 128
PAIR = 3
FLOOR2 = 0.25
REG = 1.0

OWN, NEXT, PRB, POS = 0, 2 * SR, 4 * SR, 4 * SR + 48
SEND = POS + 16
GROUP = 12

BF = jnp.bfloat16
F32 = jnp.float32
VMEM_LIMIT = 56 * 1024 * 1024


def tables():
    n = np.arange(PS, dtype=np.int64)
    angle = ((n[:, None] * n[None, :]) % PS).astype(np.float32) * np.float32(2.0 * math.pi / PS)
    c = (np.cos(angle) / np.sqrt(PS)).astype(np.float32)
    s = (np.sin(angle) / np.sqrt(PS)).astype(np.float32)
    return c, s


def table_arrays():
    c, s = tables()
    return [jnp.asarray(np.block(m).astype(jnp.bfloat16)) for m in ([[c, -s], [s, c]], [[c, s], [-s, c]])]


def pattern_kernel(first, pos_ref, cnt_ref, obj_ref, halo_ref, probe_ref, amp_ref, posblk_ref, m1_ref, m2_ref, *rest):
    if first:
        send_ref, x, pr, g, pg, patch, h, h2, amp, amp_sem = rest
    else:
        recv_ref, send_ref, objn_ref, probn_ref, x, pr, g, pg, patch, h, h2, amp, amp_sem = rest
    count = cnt_ref[0]
    copies = [pltpu.make_async_copy(amp_ref.at[j], amp.at[j], amp_sem.at[j]) for j in range(CAP)]
    for copy in copies:
        copy.start()
    tile_start = lax.axis_index("tile") * TH
    if first:
        for q in range(4):
            x[:, q, :TH, :] = obj_ref[:, :, q * LN : (q + 1) * LN]
            x[:, q, TH:, :] = halo_ref[:, :, q * LN : (q + 1) * LN].astype(F32)
        pr[...] = probe_ref[...]
    else:
        for s in range(NS):
            for k in range(2):
                a = s * SR
                new = obj_ref[k, a : a + SR, :] + recv_ref[s, k * SR : (k + 1) * SR, :].astype(F32)
                objn_ref[k, a : a + SR, :] = new
                low = halo_ref[k, a : a + SR, :].astype(F32) + recv_ref[s, (2 + k) * SR : (3 + k) * SR, :].astype(F32)
                for q in range(4):
                    x[k, q, a : a + SR, :] = new[:, q * LN : (q + 1) * LN]
                    x[k, q, TH + a : TH + a + SR, :] = low[:, q * LN : (q + 1) * LN]
                d = recv_ref[s, 4 * SR + 16 * k : 4 * SR + 16 * (k + 1), :].astype(F32)
                for q in range(2):
                    b = a + 16 * q
                    new = probe_ref[k, b : b + 16, :] + d[:, q * PS : (q + 1) * PS]
                    pr[k, b : b + 16, :] = new
                    probn_ref[k, b : b + 16, :] = new
    g[...] = jnp.zeros_like(g)
    pg[...] = jnp.zeros_like(pg)

    def place(j):
        r = pos_ref[0, j] - tile_start
        c = pos_ref[1, j]
        base = jnp.where(c >= LN, 1, 0)
        return r, base, c - base * LN

    lanes = lax.broadcasted_iota(jnp.int32, (PS, LN), 1)

    def to_half(j, slot, live):
        r, base, off = place(j)
        head = lanes < LN - off
        turn = (LN - off) & (LN - 1)
        xs = []
        for k in range(2):
            v = [pltpu.roll(x[k, base + q, pl.ds(r, PS), :], turn, 1) for q in range(3)]
            v = jnp.concatenate([jnp.where(head, v[0], v[1]), jnp.where(head, v[1], v[2])], 1)
            patch[slot, k] = v
            xs.append(v)
        xr, xi = xs
        p0, p1 = pr[0], pr[1]
        pg[2] += (xr * xr + xi * xi) * live
        w = jnp.concatenate([(p0 * xr - p1 * xi).astype(BF), (p0 * xi + p1 * xr).astype(BF)], 1)
        half = jnp.dot(w, m1_ref[...], preferred_element_type=F32).astype(BF)
        h[slot, :PS, :] = half[:, :PS]
        h[slot, PS:, :] = half[:, PS:]

    def to_back_half(j, slot, live):
        far = jnp.dot(m2_ref[...], h[slot], preferred_element_type=F32)
        fr, fi = far[:PS], far[PS:]
        m = jnp.maximum(fr * fr + fi * fi, FLOOR2)
        q = amp[j].astype(F32) * lax.rsqrt(m) - 1.0
        q = q * live
        u = jnp.concatenate([(q * fr).astype(BF), (q * fi).astype(BF)], 1)
        half = jnp.dot(u, m2_ref[...], preferred_element_type=F32).astype(BF)
        h2[slot, :PS, :] = half[:, :PS]
        h2[slot, PS:, :] = half[:, PS:]

    def add_back(j, slot):
        back = jnp.dot(m1_ref[...], h2[slot], preferred_element_type=F32)
        br, bi = back[:PS], back[PS:]
        xr, xi = patch[slot, 0], patch[slot, 1]
        pg[0] += xr * br + xi * bi
        pg[1] += xr * bi - xi * br
        p0, p1 = pr[0], pr[1]
        r, base, off = place(j)
        tail = lanes >= off
        turn = off & (LN - 1)
        for k, o in enumerate((p0 * br + p1 * bi, p0 * bi - p1 * br)):
            v = [pltpu.roll(o[:, q * LN : (q + 1) * LN], turn, 1) for q in range(2)]
            g[k, base, pl.ds(r, PS), :] += jnp.where(tail, v[0], 0.0)
            g[k, base + 1, pl.ds(r, PS), :] += jnp.where(tail, v[1], v[0])
            g[k, base + 2, pl.ds(r, PS), :] += jnp.where(tail, 0.0, v[1])

    for copy in copies:
        copy.wait()

    def visit(i, carry):
        j = [PAIR * i] + [jnp.minimum(PAIR * i + n, CAP - 1) for n in range(1, PAIR)]
        live = [jnp.where(PAIR * i + n < count, 1.0, 0.0) for n in range(PAIR)]
        for n in range(PAIR):
            to_half(j[n], n, live[n])
        for n in range(PAIR):
            to_back_half(j[n], n, live[n])
        for n in range(PAIR):
            add_back(j[n], n)
        return carry

    lax.fori_loop(0, (count + PAIR - 1) // PAIR, visit, 0)
    for s in range(NS):
        a = s * SR
        for k in range(2):
            for q in range(4):
                cols = slice(q * LN, (q + 1) * LN)
                send_ref[s, OWN + k * SR : OWN + (k + 1) * SR, cols] = g[k, q, a : a + SR, :].astype(BF)
                send_ref[s, NEXT + k * SR : NEXT + (k + 1) * SR, cols] = g[k, q, TH + a : TH + a + SR, :].astype(BF)
        for k in range(3):
            send_ref[s, PRB + 16 * k : PRB + 16 * (k + 1), :] = jnp.concatenate(
                [pg[k, a : a + 16, :], pg[k, a + 16 : a + 32, :]], 1
            ).astype(BF)
        send_ref[s, POS:, :] = posblk_ref[...]


def smem():
    return pl.BlockSpec(memory_space=pltpu.SMEM)


def vmem():
    return pl.BlockSpec(memory_space=pltpu.VMEM)


def params():
    return pltpu.CompilerParams(vmem_limit_bytes=VMEM_LIMIT)


def patterns(pos, cnt, obj, halo, probe, amps, posblk, tabs, recv=None):
    first = recv is None
    out = [jax.ShapeDtypeStruct((NS, SEND, OW), BF)]
    if not first:
        out += [jax.ShapeDtypeStruct((2, TH, OW), F32), jax.ShapeDtypeStruct((2, PS, PS), F32)]
    args = [pos, cnt, obj, halo, probe, amps, posblk, *tabs] + ([] if first else [recv])
    return pl.pallas_call(
        functools.partial(pattern_kernel, first),
        out_shape=out,
        in_specs=[smem(), smem()] + [vmem()] * 3 + [pl.BlockSpec(memory_space=pl.ANY)] + [vmem()] * (len(args) - 6),
        out_specs=[vmem()] * len(out),
        scratch_shapes=[
            pltpu.VMEM((2, 4, 2 * TH, LN), F32),
            pltpu.VMEM((2, PS, PS), F32),
            pltpu.VMEM((2, 4, 2 * TH, LN), F32),
            pltpu.VMEM((3, PS, PS), F32),
            pltpu.VMEM((PAIR, 2, PS, PS), F32),
            pltpu.VMEM((PAIR, 2 * PS, PS), BF),
            pltpu.VMEM((PAIR, 2 * PS, PS), BF),
            pltpu.VMEM((CAP, PS, PS), BF),
            pltpu.SemaphoreType.DMA((CAP,)),
        ],
        compiler_params=params(),
        name="patterns",
    )(*args)


def odd_tile():
    return lax.rem(lax.axis_index("tile"), 2) == 1


def sum_kernel(last, recv_ref, own_ref, next_ref, probe_ref, *rest):
    def total(a, n):
        t = recv_ref[0, a : a + n, :].astype(F32)
        for s in range(1, NS):
            t = t + recv_ref[s, a : a + n, :].astype(F32)
        return t

    own = total(OWN, 2 * SR)
    own_ref[...] = own
    nxt = total(NEXT, 2 * SR)
    next_ref[...] = nxt
    probe_ref[...] = total(PRB, 48).astype(BF)
    if last:
        (up_ref,) = rest
        up_ref[...] = nxt.astype(BF)
    else:
        inner_ref, outer_ref, pos_ref = rest
        odd = odd_tile()
        pos = total(POS, 16)
        pos_ref[...] = pos[:, :LN]
        inner_ref[: 2 * SR, :] = jnp.where(odd, own, nxt).astype(BF)
        outer_ref[: 2 * SR, :] = jnp.where(odd, nxt, own).astype(BF)
        inner_ref[2 * SR :, :] = pos.astype(BF)
        outer_ref[2 * SR :, :] = pos.astype(BF)


def sums(last, recv):
    out = [
        jax.ShapeDtypeStruct((2 * SR, OW), F32),
        jax.ShapeDtypeStruct((2 * SR, OW), F32),
        jax.ShapeDtypeStruct((48, OW), BF),
    ]
    if last:
        out += [jax.ShapeDtypeStruct((2 * SR, OW), BF)]
    else:
        out += [jax.ShapeDtypeStruct((2 * SR + 16, OW), BF)] * 2 + [jax.ShapeDtypeStruct((16, LN), F32)]
    return pl.pallas_call(
        functools.partial(sum_kernel, last),
        out_shape=out,
        in_specs=[vmem()],
        out_specs=[vmem()] * len(out),
        compiler_params=params(),
        name="sums",
    )(recv)


def illum_kernel(last, pos_ref, probe_ref, out_ref, p2):
    for q in range(2):
        cols = slice(q * LN, (q + 1) * LN)
        p2[q, :SR, :] = jnp.zeros((SR, LN), F32)
        p2[q, SR + PS :, :] = jnp.zeros((SR, LN), F32)
        p2[q, SR : SR + PS, :] = probe_ref[0, :, cols] * probe_ref[0, :, cols] + probe_ref[1, :, cols] * probe_ref[1, :, cols]
    mine = lax.axis_index("scan") * SR
    lanes = lax.broadcasted_iota(jnp.int32, (SR, LN), 1)
    zero = jnp.zeros((SR, LN), F32)

    def add(shift, blocks, carry):
        def group(s, carry):
            row = (shift + 1) * NS + s

            def some(i, carry):
                carry = [list(c) for c in carry]
                for n in range(4):
                    j = 4 * i + n
                    code = pos_ref[row, j]
                    first = jnp.where(code > 0, code + (shift * TH - 1), -4 * TH)
                    c = pos_ref[row, GROUP + j]
                    turn = c & (LN - 1)
                    masks = [lanes >= c - q * LN for q in range(4)]
                    ends = [lanes >= c + (2 - q) * LN for q in range(4)]
                    left = [lanes >= c + (1 - q) * LN for q in range(4)]
                    for b in blocks:
                        at = jnp.clip(mine + b * TH - first, -SR, PS) + SR
                        y0, y1 = (pltpu.roll(p2[q, pl.ds(at, SR), :], turn, 1) for q in range(2))
                        for q in range(4):
                            v = jnp.where(masks[q], jnp.where(left[q], jnp.where(ends[q], 0.0, y1), y0), 0.0)
                            carry[b][q] = carry[b][q] + v
                return tuple(tuple(c) for c in carry)

            return lax.fori_loop(0, (pos_ref[row, 2 * GROUP] + 3) // 4, some, carry)

        return lax.fori_loop(0, NS, group, carry)

    carry = tuple((zero,) * 4 for _ in range(1 if last else 2))
    carry = add(-1, (0,), carry)
    carry = add(0, (0,) if last else (0, 1), carry)
    if not last:
        carry = add(1, (1,), carry)
    for block, values in enumerate(carry):
        for q in range(4):
            out_ref[block, :, q * LN : (q + 1) * LN] = values[q]


def illumination(last, pos, probe):
    return pl.pallas_call(
        functools.partial(illum_kernel, last),
        out_shape=jax.ShapeDtypeStruct((1 if last else 2, SR, OW), F32),
        in_specs=[smem(), vmem()],
        out_specs=vmem(),
        scratch_shapes=[pltpu.VMEM((2, PS + 2 * SR, LN), F32)],
        compiler_params=params(),
        name="illumination",
    )(pos, probe)


def step_kernel(last, *refs):
    if last:
        own_ref, up_ref, ill_ref, p0_ref, p1_ref, out_ref = refs
        up = up_ref[...].astype(F32)
    else:
        own_ref, next_ref, inner_ref, outer_ref, ill_ref, p0_ref, p1_ref, out_ref = refs
        odd = odd_tile()
        inner = inner_ref[: 2 * SR, :].astype(F32)
        outer = outer_ref[: 2 * SR, :].astype(F32)
        up = jnp.where(odd, inner, outer)
        down = jnp.where(odd, outer, inner)
    probe = p0_ref[...].astype(F32) + p1_ref[...].astype(F32)
    w = probe[32:] + REG
    parts = []
    for k in range(2):
        a = k * SR
        parts.append((own_ref[a : a + SR, :] + up[a : a + SR, :]) / (ill_ref[0] + REG))
    if last:
        root = jnp.sqrt(w)
        parts += [probe[:16] / root, probe[16:32] / root, root]
    else:
        for k in range(2):
            a = k * SR
            parts.append((next_ref[a : a + SR, :] + down[a : a + SR, :]) / (ill_ref[1] + REG))
        parts += [probe[:16] / w, probe[16:32] / w]
    at = 0
    for part in parts:
        n = part.shape[0]
        part = part.astype(BF)
        for s in range(NS):
            out_ref[s, at : at + n, :] = part
        at += n


def steps(last, *args):
    rows = 2 * SR + 48 if last else 4 * SR + 32
    return pl.pallas_call(
        functools.partial(step_kernel, last),
        out_shape=jax.ShapeDtypeStruct((NS, rows, OW), BF),
        in_specs=[vmem()] * len(args),
        out_specs=vmem(),
        compiler_params=params(),
        name="steps",
    )(*args)


def final_kernel(obj_ref, probe_ref, recv_ref, obj_out, probe_out, grad_out):
    for s in range(NS):
        a = s * SR
        root = recv_ref[s, 2 * SR + 32 : 2 * SR + 48, :].astype(F32)
        for k in range(2):
            obj_out[k, a : a + SR, :] = obj_ref[k, a : a + SR, :] + recv_ref[s, k * SR : (k + 1) * SR, :].astype(F32)
            grad = recv_ref[s, 2 * SR + 16 * k : 2 * SR + 16 * (k + 1), :].astype(F32)
            d = grad / root
            for q in range(2):
                b = a + 16 * q
                grad_out[k, b : b + 16, :] = grad[:, q * PS : (q + 1) * PS]
                probe_out[k, b : b + 16, :] = probe_ref[k, b : b + 16, :] + d[:, q * PS : (q + 1) * PS]


def final(obj, probe, recv):
    return pl.pallas_call(
        final_kernel,
        out_shape=[
            jax.ShapeDtypeStruct((2, TH, OW), F32),
            jax.ShapeDtypeStruct((2, PS, PS), F32),
            jax.ShapeDtypeStruct((2, PS, PS), F32),
        ],
        in_specs=[vmem()] * 3,
        out_specs=[vmem()] * 3,
        compiler_params=params(),
        name="final",
    )(obj, probe, recv)


def shifted(block, distance):
    return lax.ppermute(block, "tile", [(i, i + distance) for i in range(NT) if 0 <= i + distance < NT])


def swapped(block, bits):
    return lax.ppermute(block, "tile", [(i, i ^ bits) for i in range(NT)])


def four(x, swaps):
    y = [swap.astype(F32) for swap in swaps]
    return ((x.astype(F32) + y[0]) + (y[1] + y[2])).astype(BF)


def exchange(blocks):
    return lax.all_to_all(blocks, "scan", 0, 0, tiled=True)


def on_device(object_field, probe, amplitudes, positions, counts):
    tabs = table_arrays()
    pos = positions[0, 0].T
    cnt = counts[0, 0].reshape(1)
    amps = amplitudes[0, 0]
    halo = shifted(object_field.astype(BF), -1)
    live = lax.broadcasted_iota(jnp.int32, (CAP,), 0) < cnt
    row = jnp.concatenate([jnp.where(live, pos[0] - lax.axis_index("tile") * TH + 1, 0), pos[1], cnt])
    mine = lax.broadcasted_iota(jnp.int32, (16, 1), 0) == lax.axis_index("scan")
    posblk = jnp.where(mine, row[None, :], 0).astype(BF)
    posblk = jnp.pad(posblk, ((0, 0), (0, OW - row.shape[0])))
    coded = 2 * GROUP + 1
    (send,) = patterns(pos, cnt, object_field, halo, probe, amps, posblk, tabs)
    own, nxt, part, inner, outer, tile_pos = sums(False, exchange(send))
    swaps = [swapped(part, 1), swapped(part, 2), swapped(part, 3)]
    inner = swapped(inner, 1)
    outer = lax.ppermute(outer, "tile", [(i, i + 1 if i % 2 else i - 1) for i in range(1, NT - 1)])
    part = four(part, swaps)
    swaps = [swapped(part, 4), swapped(part, 8), swapped(part, 12)]
    odd = odd_tile()
    above = jnp.where(odd, inner[2 * SR :, :coded], outer[2 * SR :, :coded])[:NS]
    below = jnp.where(odd, outer[2 * SR :, :coded], inner[2 * SR :, :coded])[:NS]
    around = jnp.concatenate([above.astype(F32), tile_pos[:NS, :coded], below.astype(F32)], 0).astype(jnp.int32)
    ill = illumination(False, around, probe)
    part, ill = lax.optimization_barrier((four(part, swaps), ill))
    other = swapped(part, 16)
    recv = exchange(steps(False, own, nxt, inner, outer, ill, part, other))
    send, object_field, probe = patterns(pos, cnt, object_field, halo, probe, amps, posblk, tabs, recv)
    own, nxt, part, up = sums(True, exchange(send))
    swaps = [swapped(part, 1), swapped(part, 2), swapped(part, 3)]
    up = shifted(up, 1)
    ill = illumination(True, around, probe)
    part, ill = lax.optimization_barrier((four(part, swaps), ill))
    swaps = [swapped(part, 4), swapped(part, 8), swapped(part, 12)]
    part = four(part, swaps)
    other = swapped(part, 16)
    recv = exchange(steps(True, own, up, ill, part, other))
    return tuple(final(object_field, probe, recv))


def solution(mesh):
    in_specs = (
        P(None, "tile", None),
        P(),
        P("scan", "tile", None, None, None),
        P("scan", "tile", None, None),
        P("scan", "tile"),
    )
    out_specs = (P(None, "tile", None), P(), P())
    return jax.shard_map(on_device, mesh=mesh, in_specs=in_specs, out_specs=out_specs, check_vma=False)
```

profile of v0, /device:TPU:8, one launch (start us, length us, event | category | flops | bytes accessed | tf_op | source)
XLA Modules:
  0.0 193.5 jit_solution(1103979547653127725)
XLA Ops:
  0.6 1.3 convert_element_type.77
  1.9 7.1 %collective-permute-start = (bf16[2,256,512]{2,1,0:T(8,128)(2,1)S(1)}, bf16[2,256,512]{2,1,0:T(8,128)(2,1)S(1)}, u32[]{:S(2)}, u32[]{:S(2)}) collective-permute-start(bf16[2,256,512]{2,1,0:T(8,128)(2,1)S(1)} %convert_element_type.77), channel_id=1, source_target_pairs={{1,0},{2,1},{3,2},{4,3},{5,4},{6,5},{7,6},{8,7},{9,8},{10,9},{11,1... | collective-permute-start | bytes 1572872 | tf_op jit(solution)/shard_map/ppermute | solution.py:387
  10.5 5.2 %collective-permute-done.halo_ref = bf16[2,256,512]{2,1,0:T(8,128)(2,1)S(1)} collective-permute-done((bf16[2,256,512]{2,1,0:T(8,128)(2,1)S(1)}, bf16[2,256,512]{2,1,0:T(8,128)(2,1)S(1)}, u32[]{:S(2)}, u32[]{:S(2)}) %collective-permute-start) | collective-permute-done | bytes 524320 | tf_op jit(solution)/shard_map/ppermute | solution.py:387
  15.7 0.8 copy-done
  16.5 7.8 %patterns.2 = bf16[8,192,512]{2,1,0:T(8,128)(2,1)} custom-call(s32[2,12]{1,0:T(2,128)} %bitcast.16, s32[1]{0:T(128)} %bitcast.11.cnt_ref, f32[2,256,512]{2,1,0:T(8,128)} %obj_ref.3, bf16[2,256,512]{2,1,0:T(8,128)(2,1)} %copy-done, f32[2,256,256]{2,1,0:T(8,128)} %probe_ref.5, bf16[12,256,256]{2,1,0:T(8,128)(2,1)} %bitcast.14, bf16[16,512]{1,0:T(8,128)(2,1)} %pad.4.posblk_ref, ...), custom_call_target="tpu_custom_call" | custom-call | tf_op jit(solution)/shard_map/patterns/pallas_call | solution.py:181
  24.3 29.5 %all_to_all.20.recv_ref = bf16[8,192,512]{2,1,0:T(8,128)(2,1)} all-to-all(bf16[8,192,512]{2,1,0:T(8,128)(2,1)} %patterns.2), channel_id=1, replica_groups=mesh['scan'=8,'tile'=32] {'scan'}, dimensions={0} | all-to-all | bytes 3145728 | tf_op jit(solution)/shard_map/all_to_all | solution.py:400
  53.8 2.3 %sums.2 = (f32[64,512]{1,0:T(8,128)}, f32[64,512]{1,0:T(8,128)}, bf16[48,512]{1,0:T(8,128)(2,1)}, bf16[80,512]{1,0:T(8,128)(2,1)}, bf16[80,512]{1,0:T(8,128)(2,1)}, /*index=5*/f32[16,128]{1,0:T(8,128)}) custom-call(bf16[8,192,512]{2,1,0:T(8,128)(2,1)} %all_to_all.20.recv_ref), custom_call_target="tpu_custom_call" | custom-call | tf_op jit(solution)/shard_map/sums/pallas_call | solution.py:242
  56.2 1.8 collective-permute-start.3
  58.6 6.6 %collective-permute-start.2 = (bf16[80,512]{1,0:T(8,128)(2,1)}, bf16[80,512]{1,0:T(8,128)(2,1)S(1)}, u32[]{:S(2)}, u32[]{:S(2)}) collective-permute-start(bf16[80,512]{1,0:T(8,128)(2,1)} %get-tuple-element.22), channel_id=1, source_target_pairs={{1,2},{2,1},{3,4},{4,3},{5,6},{6,5},{7,8},{8,7},{9,10},{10,9},{11,... | collective-permute-start | bytes 245768 | tf_op jit(solution)/shard_map/ppermute | solution.py:419
  65.3 0.8 add_convert_fusion.3
  66.2 0.7 collective-permute-start.7
  66.9 5.8 %collective-permute-start.6 = (bf16[48,512]{1,0:T(8,128)(2,1)S(1)}, bf16[48,512]{1,0:T(8,128)(2,1)S(1)}, u32[]{:S(2)}, u32[]{:S(2)}) collective-permute-start(bf16[48,512]{1,0:T(8,128)(2,1)S(1)} %add_convert_fusion.3), channel_id=1, source_target_pairs={{0,4},{1,5},{2,6},{3,7},{4,0},{5,1},{6,2},{7,3},{8,12},{9,13},{10,... | collective-permute-start | bytes 147464 | tf_op jit(solution)/shard_map/ppermute | solution.py:391
  73.4 6.3 %illumination.2.refs_4_ = f32[2,32,512]{2,1,0:T(8,128)} custom-call(s32[24,25]{1,0:T(8,128)} %maximum_convert_fusion.pos_ref, f32[2,256,256]{2,1,0:T(8,128)} %probe_ref.5), custom_call_target="tpu_custom_call" | custom-call | tf_op jit(solution)/shard_map/illumination/pallas_call | solution.py:300
  79.8 4.1 %collective-permute-done.9.refs_6_ = bf16[48,512]{1,0:T(8,128)(2,1)S(1)} collective-permute-done((bf16[48,512]{1,0:T(8,128)(2,1)S(1)}, bf16[48,512]{1,0:T(8,128)(2,1)S(1)}, u32[]{:S(2)}, u32[]{:S(2)}) %collective-permute-start.9) | collective-permute-done | bytes 49184 | tf_op jit(solution)/shard_map/ppermute | solution.py:391
  84.5 2.3 %steps.2 = bf16[8,160,512]{2,1,0:T(8,128)(2,1)} custom-call(f32[64,512]{1,0:T(8,128)} %get-tuple-element.19.refs_0_, f32[64,512]{1,0:T(8,128)} %get-tuple-element.20.refs_1_, bf16[80,512]{1,0:T(8,128)(2,1)} %copy-done.3, bf16[80,512]{1,0:T(8,128)(2,1)} %copy-done.4, f32[2,32,512]{2,1,0:T(8,128)} %illumination.2.refs_4_, bf16[48,512]{1,0:T(8,128)(2,1)} %copy-done.2, ...), custom_call_target="tpu_custom_call" | custom-call | tf_op jit(solution)/shard_map/steps/pallas_call | solution.py:347
  86.9 18.7 %all_to_all.21.rest_0_ = bf16[8,160,512]{2,1,0:T(8,128)(2,1)} all-to-all(bf16[8,160,512]{2,1,0:T(8,128)(2,1)} %steps.2), channel_id=1, replica_groups=mesh['scan'=8,'tile'=32] {'scan'}, dimensions={0} | all-to-all | bytes 2621440 | tf_op jit(solution)/shard_map/all_to_all | solution.py:400
  105.6 8.6 %patterns.3 = (bf16[8,192,512]{2,1,0:T(8,128)(2,1)}, f32[2,256,512]{2,1,0:T(8,128)}, f32[2,256,256]{2,1,0:T(8,128)}) custom-call(s32[2,12]{1,0:T(2,128)} %bitcast.17, s32[1]{0:T(128)} %bitcast.12.cnt_ref, f32[2,256,512]{2,1,0:T(8,128)} %obj_ref.3, bf16[2,256,512]{2,1,0:T(8,128)(2,1)} %copy-done, f32[2,256,256]{2,1,0:T(8,128)} %probe_ref.5, ...), custom_call_target="tpu_custom_call" | custom-call | tf_op jit(solution)/shard_map/patterns/pallas_call | solution.py:181
  114.2 24.8 %all_to_all.22.recv_ref = bf16[8,192,512]{2,1,0:T(8,128)(2,1)} all-to-all(bf16[8,192,512]{2,1,0:T(8,128)(2,1)} %get-tuple-element.29), channel_id=1, replica_groups=mesh['scan'=8,'tile'=32] {'scan'}, dimensions={0} | all-to-all | bytes 3145728 | tf_op jit(solution)/shard_map/all_to_all | solution.py:400
  139.0 2.2 %sums.3 = (f32[64,512]{1,0:T(8,128)}, f32[64,512]{1,0:T(8,128)}, bf16[48,512]{1,0:T(8,128)(2,1)}, bf16[64,512]{1,0:T(8,128)(2,1)}) custom-call(bf16[8,192,512]{2,1,0:T(8,128)(2,1)} %all_to_all.22.recv_ref), custom_call_target="tpu_custom_call" | custom-call | tf_op jit(solution)/shard_map/sums/pallas_call | solution.py:242
  141.2 2.2 %collective-permute-start.13 = (bf16[48,512]{1,0:T(8,128)(2,1)}, bf16[48,512]{1,0:T(8,128)(2,1)S(1)}, u32[]{:S(2)}, u32[]{:S(2)}) collective-permute-start(bf16[48,512]{1,0:T(8,128)(2,1)} %get-tuple-element.32), channel_id=1, source_target_pairs={{0,3},{1,2},{2,1},{3,0},{4,7},{5,6},{6,5},{7,4},{8,11},{9,10},{10,... | collective-permute-start | bytes 147464 | tf_op jit(solution)/shard_map/ppermute | solution.py:391
  143.5 2.5 %collective-permute-start.12 = (bf16[48,512]{1,0:T(8,128)(2,1)}, bf16[48,512]{1,0:T(8,128)(2,1)S(1)}, u32[]{:S(2)}, u32[]{:S(2)}) collective-permute-start(bf16[48,512]{1,0:T(8,128)(2,1)} %get-tuple-element.32), channel_id=1, source_target_pairs={{0,2},{1,3},{2,0},{3,1},{4,6},{5,7},{6,4},{7,5},{8,10},{9,11},{10,... | collective-permute-start | bytes 147464 | tf_op jit(solution)/shard_map/ppermute | solution.py:391
  146.0 4.1 %illumination.3.refs_2_ = f32[1,32,512]{2,1,0:T(8,128)} custom-call(s32[24,25]{1,0:T(8,128)} %maximum_convert_fusion.pos_ref, f32[2,256,256]{2,1,0:T(8,128)} %get-tuple-element.28.probe_ref), custom_call_target="tpu_custom_call" | custom-call | tf_op jit(solution)/shard_map/illumination/pallas_call | solution.py:300
  150.2 0.8 add_convert_fusion.1
  151.1 5.6 %collective-permute-start.15 = (bf16[48,512]{1,0:T(8,128)(2,1)S(1)}, bf16[48,512]{1,0:T(8,128)(2,1)S(1)}, u32[]{:S(2)}, u32[]{:S(2)}) collective-permute-start(bf16[48,512]{1,0:T(8,128)(2,1)S(1)} %add_convert_fusion.1), channel_id=1, source_target_pairs={{0,8},{1,9},{2,10},{3,11},{4,12},{5,13},{6,14},{7,15},{8,0},{9,1},... | collective-permute-start | bytes 147464 | tf_op jit(solution)/shard_map/ppermute | solution.py:391
  156.6 0.9 collective-permute-start.14
  157.6 2.1 %collective-permute-start.10 = (bf16[64,512]{1,0:T(8,128)(2,1)}, bf16[64,512]{1,0:T(8,128)(2,1)S(1)}, u32[]{:S(2)}, u32[]{:S(2)}) collective-permute-start(bf16[64,512]{1,0:T(8,128)(2,1)} %get-tuple-element.31), channel_id=1, source_target_pairs={{0,1},{1,2},{2,3},{3,4},{4,5},{5,6},{6,7},{7,8},{8,9},{9,10},{10,1... | collective-permute-start | bytes 196616 | tf_op jit(solution)/shard_map/ppermute | solution.py:387
  160.2 3.2 %collective-permute-done.14 = bf16[48,512]{1,0:T(8,128)(2,1)S(1)} collective-permute-done((bf16[48,512]{1,0:T(8,128)(2,1)S(1)}, bf16[48,512]{1,0:T(8,128)(2,1)S(1)}, u32[]{:S(2)}, u32[]{:S(2)}) %collective-permute-start.14) | collective-permute-done | bytes 49184 | tf_op jit(solution)/shard_map/ppermute | solution.py:391
  163.5 2.9 %collective-permute-start.17 = (bf16[48,512]{1,0:T(8,128)(2,1)S(1)}, bf16[48,512]{1,0:T(8,128)(2,1)S(1)}, u32[]{:S(2)}, u32[]{:S(2)}) collective-permute-start(bf16[48,512]{1,0:T(8,128)(2,1)S(1)} %add_convert_fusion.refs_3_), channel_id=1, source_target_pairs={{0,16},{1,17},{2,18},{3,19},{4,20},{5,21},{6,22},{7,23},{8,24},{9,... | collective-permute-start | bytes 147464 | tf_op jit(solution)/shard_map/ppermute | solution.py:391
  166.4 2.1 %collective-permute-done.17.refs_4_ = bf16[48,512]{1,0:T(8,128)(2,1)S(1)} collective-permute-done((bf16[48,512]{1,0:T(8,128)(2,1)S(1)}, bf16[48,512]{1,0:T(8,128)(2,1)S(1)}, u32[]{:S(2)}, u32[]{:S(2)}) %collective-permute-start.17) | collective-permute-done | bytes 49184 | tf_op jit(solution)/shard_map/ppermute | solution.py:391
  169.1 2.0 %steps.3 = bf16[8,112,512]{2,1,0:T(8,128)(2,1)} custom-call(f32[64,512]{1,0:T(8,128)} %get-tuple-element.30.refs_0_, bf16[64,512]{1,0:T(8,128)(2,1)} %copy-done.5, f32[1,32,512]{2,1,0:T(8,128)} %illumination.3.refs_2_, bf16[48,512]{1,0:T(8,128)(2,1)} %copy-done.1, bf16[48,512]{1,0:T(8,128)(2,1)} %copy-done.6), custom_call_target="tpu_custom_call" | custom-call | tf_op jit(solution)/shard_map/steps/pallas_call | solution.py:347
  171.1 19.4 %all_to_all.23.recv_ref = bf16[8,112,512]{2,1,0:T(8,128)(2,1)} all-to-all(bf16[8,112,512]{2,1,0:T(8,128)(2,1)} %steps.3), channel_id=1, replica_groups=mesh['scan'=8,'tile'=32] {'scan'}, dimensions={0} | all-to-all | bytes 1835008 | tf_op jit(solution)/shard_map/all_to_all | solution.py:400
  190.4 3.0 %final.1 = (f32[2,256,512]{2,1,0:T(8,128)}, f32[2,256,256]{2,1,0:T(8,128)}, f32[2,256,256]{2,1,0:T(8,128)}) custom-call(f32[2,256,512]{2,1,0:T(8,128)} %get-tuple-element.27.obj_ref, f32[2,256,256]{2,1,0:T(8,128)} %get-tuple-element.28.probe_ref, bf16[8,112,512]{2,1,0:T(8,128)(2,1)} %all_to_all.23.recv_ref), custom_call_target="tpu_custom_call" | custom-call | tf_op jit(solution)/shard_map/final/pallas_call | solution.py:372
  (51 shorter events, 4.4 us)
Async XLA Ops:
  0.6 9.1 %copy-start.8 = (s32[1,1,12,2]{2,3,1,0:T(2,128)S(1)}, s32[1,1,12,2]{2,3,1,0:T(2,128)}, u32[]{:S(2)}) copy-start(s32[1,1,12,2]{2,3,1,0:T(2,128)} %param.10) | copy-start | bytes 292
  1.9 13.8 %collective-permute-start = (bf16[2,256,512]{2,1,0:T(8,128)(2,1)S(1)}, bf16[2,256,512]{2,1,0:T(8,128)(2,1)S(1)}, u32[]{:S(2)}, u32[]{:S(2)}) collective-permute-start(bf16[2,256,512]{2,1,0:T(8,128)(2,1)S(1)} %convert_element_type.77), channel_id=1, source_target_pairs={{1,0},{2,1},{3,2},{4,3},{5,4},{6,5},{7,6},{8,7},{9,8},{10,9},{11,1... | collective-permute-start | bytes 1572872 | tf_op jit(solution)/shard_map/ppermute | solution.py:387
  15.7 0.8 copy-start
  56.1 9.1 %collective-permute-start.5 = (bf16[48,512]{1,0:T(8,128)(2,1)}, bf16[48,512]{1,0:T(8,128)(2,1)S(1)}, u32[]{:S(2)}, u32[]{:S(2)}) collective-permute-start(bf16[48,512]{1,0:T(8,128)(2,1)} %get-tuple-element.23), channel_id=1, source_target_pairs={{0,3},{1,2},{2,1},{3,0},{4,7},{5,6},{6,5},{7,4},{8,11},{9,10},{10,... | collective-permute-start | bytes 147464 | tf_op jit(solution)/shard_map/ppermute | solution.py:391
  56.1 9.2 %collective-permute-start.4 = (bf16[48,512]{1,0:T(8,128)(2,1)}, bf16[48,512]{1,0:T(8,128)(2,1)S(1)}, u32[]{:S(2)}, u32[]{:S(2)}) collective-permute-start(bf16[48,512]{1,0:T(8,128)(2,1)} %get-tuple-element.23), channel_id=1, source_target_pairs={{0,2},{1,3},{2,0},{3,1},{4,6},{5,7},{6,4},{7,5},{8,10},{9,11},{10,... | collective-permute-start | bytes 147464 | tf_op jit(solution)/shard_map/ppermute | solution.py:391
  56.2 9.1 %collective-permute-start.3 = (bf16[48,512]{1,0:T(8,128)(2,1)}, bf16[48,512]{1,0:T(8,128)(2,1)S(1)}, u32[]{:S(2)}, u32[]{:S(2)}) collective-permute-start(bf16[48,512]{1,0:T(8,128)(2,1)} %get-tuple-element.23), channel_id=1, source_target_pairs={{0,1},{1,0},{2,3},{3,2},{4,5},{5,4},{6,7},{7,6},{8,9},{9,8},{10,11... | collective-permute-start | bytes 147464 | tf_op jit(solution)/shard_map/ppermute | solution.py:391
  58.6 14.1 %collective-permute-start.1 = (bf16[80,512]{1,0:T(8,128)(2,1)}, bf16[80,512]{1,0:T(8,128)(2,1)S(1)}, u32[]{:S(2)}, u32[]{:S(2)}) collective-permute-start(bf16[80,512]{1,0:T(8,128)(2,1)} %get-tuple-element.21), channel_id=1, source_target_pairs={{0,1},{1,0},{2,3},{3,2},{4,5},{5,4},{6,7},{7,6},{8,9},{9,8},{10,11... | collective-permute-start | bytes 245768 | tf_op jit(solution)/shard_map/ppermute | solution.py:391
  58.6 14.1 %collective-permute-start.2 = (bf16[80,512]{1,0:T(8,128)(2,1)}, bf16[80,512]{1,0:T(8,128)(2,1)S(1)}, u32[]{:S(2)}, u32[]{:S(2)}) collective-permute-start(bf16[80,512]{1,0:T(8,128)(2,1)} %get-tuple-element.22), channel_id=1, source_target_pairs={{1,2},{2,1},{3,4},{4,3},{5,6},{6,5},{7,8},{8,7},{9,10},{10,9},{11,... | collective-permute-start | bytes 245768 | tf_op jit(solution)/shard_map/ppermute | solution.py:419
  66.1 13.6 %collective-permute-start.8 = (bf16[48,512]{1,0:T(8,128)(2,1)S(1)}, bf16[48,512]{1,0:T(8,128)(2,1)S(1)}, u32[]{:S(2)}, u32[]{:S(2)}) collective-permute-start(bf16[48,512]{1,0:T(8,128)(2,1)S(1)} %add_convert_fusion.3), channel_id=1, source_target_pairs={{0,12},{1,13},{2,14},{3,15},{4,8},{5,9},{6,10},{7,11},{8,4},{9,5},... | collective-permute-start | bytes 147464 | tf_op jit(solution)/shard_map/ppermute | solution.py:391
  66.2 13.5 %collective-permute-start.7 = (bf16[48,512]{1,0:T(8,128)(2,1)S(1)}, bf16[48,512]{1,0:T(8,128)(2,1)S(1)}, u32[]{:S(2)}, u32[]{:S(2)}) collective-permute-start(bf16[48,512]{1,0:T(8,128)(2,1)S(1)} %add_convert_fusion.3), channel_id=1, source_target_pairs={{0,8},{1,9},{2,10},{3,11},{4,12},{5,13},{6,14},{7,15},{8,0},{9,1},... | collective-permute-start | bytes 147464 | tf_op jit(solution)/shard_map/ppermute | solution.py:391
  66.9 12.7 %collective-permute-start.6 = (bf16[48,512]{1,0:T(8,128)(2,1)S(1)}, bf16[48,512]{1,0:T(8,128)(2,1)S(1)}, u32[]{:S(2)}, u32[]{:S(2)}) collective-permute-start(bf16[48,512]{1,0:T(8,128)(2,1)S(1)} %add_convert_fusion.3), channel_id=1, source_target_pairs={{0,4},{1,5},{2,6},{3,7},{4,0},{5,1},{6,2},{7,3},{8,12},{9,13},{10,... | collective-permute-start | bytes 147464 | tf_op jit(solution)/shard_map/ppermute | solution.py:391
  72.7 11.2 %copy-start.3 = (bf16[80,512]{1,0:T(8,128)(2,1)}, bf16[80,512]{1,0:T(8,128)(2,1)S(1)}, u32[]{:S(2)}) copy-start(bf16[80,512]{1,0:T(8,128)(2,1)S(1)} %collective-permute-done.1.refs_2_) | copy-start | bytes 245764
  72.7 11.2 %copy-start.4 = (bf16[80,512]{1,0:T(8,128)(2,1)}, bf16[80,512]{1,0:T(8,128)(2,1)S(1)}, u32[]{:S(2)}) copy-start(bf16[80,512]{1,0:T(8,128)(2,1)S(1)} %collective-permute-done.2.refs_3_) | copy-start | bytes 245764
  79.7 4.2 %copy-start.2 = (bf16[48,512]{1,0:T(8,128)(2,1)}, bf16[48,512]{1,0:T(8,128)(2,1)S(1)}, u32[]{:S(2)}) copy-start(bf16[48,512]{1,0:T(8,128)(2,1)S(1)} %add_convert_fusion.2.refs_5_) | copy-start | bytes 147460
  79.7 4.2 %collective-permute-start.9 = (bf16[48,512]{1,0:T(8,128)(2,1)S(1)}, bf16[48,512]{1,0:T(8,128)(2,1)S(1)}, u32[]{:S(2)}, u32[]{:S(2)}) collective-permute-start(bf16[48,512]{1,0:T(8,128)(2,1)S(1)} %add_convert_fusion.2.refs_5_), channel_id=1, source_target_pairs={{0,16},{1,17},{2,18},{3,19},{4,20},{5,21},{6,22},{7,23},{8,24},{9,... | collective-permute-start | bytes 147464 | tf_op jit(solution)/shard_map/ppermute | solution.py:391
  83.9 0.6 copy-start.7
  141.2 8.9 %collective-permute-start.13 = (bf16[48,512]{1,0:T(8,128)(2,1)}, bf16[48,512]{1,0:T(8,128)(2,1)S(1)}, u32[]{:S(2)}, u32[]{:S(2)}) collective-permute-start(bf16[48,512]{1,0:T(8,128)(2,1)} %get-tuple-element.32), channel_id=1, source_target_pairs={{0,3},{1,2},{2,1},{3,0},{4,7},{5,6},{6,5},{7,4},{8,11},{9,10},{10,... | collective-permute-start | bytes 147464 | tf_op jit(solution)/shard_map/ppermute | solution.py:391
  143.5 6.7 %collective-permute-start.12 = (bf16[48,512]{1,0:T(8,128)(2,1)}, bf16[48,512]{1,0:T(8,128)(2,1)S(1)}, u32[]{:S(2)}, u32[]{:S(2)}) collective-permute-start(bf16[48,512]{1,0:T(8,128)(2,1)} %get-tuple-element.32), channel_id=1, source_target_pairs={{0,2},{1,3},{2,0},{3,1},{4,6},{5,7},{6,4},{7,5},{8,10},{9,11},{10,... | collective-permute-start | bytes 147464 | tf_op jit(solution)/shard_map/ppermute | solution.py:391
  146.0 4.2 %collective-permute-start.11 = (bf16[48,512]{1,0:T(8,128)(2,1)}, bf16[48,512]{1,0:T(8,128)(2,1)S(1)}, u32[]{:S(2)}, u32[]{:S(2)}) collective-permute-start(bf16[48,512]{1,0:T(8,128)(2,1)} %get-tuple-element.32), channel_id=1, source_target_pairs={{0,1},{1,0},{2,3},{3,2},{4,5},{5,4},{6,7},{7,6},{8,9},{9,8},{10,11... | collective-permute-start | bytes 147464 | tf_op jit(solution)/shard_map/ppermute | solution.py:391
  151.0 8.7 %collective-permute-start.16 = (bf16[48,512]{1,0:T(8,128)(2,1)S(1)}, bf16[48,512]{1,0:T(8,128)(2,1)S(1)}, u32[]{:S(2)}, u32[]{:S(2)}) collective-permute-start(bf16[48,512]{1,0:T(8,128)(2,1)S(1)} %add_convert_fusion.1), channel_id=1, source_target_pairs={{0,12},{1,13},{2,14},{3,15},{4,8},{5,9},{6,10},{7,11},{8,4},{9,5},... | collective-permute-start | bytes 147464 | tf_op jit(solution)/shard_map/ppermute | solution.py:391
  151.1 9.1 %collective-permute-start.15 = (bf16[48,512]{1,0:T(8,128)(2,1)S(1)}, bf16[48,512]{1,0:T(8,128)(2,1)S(1)}, u32[]{:S(2)}, u32[]{:S(2)}) collective-permute-start(bf16[48,512]{1,0:T(8,128)(2,1)S(1)} %add_convert_fusion.1), channel_id=1, source_target_pairs={{0,8},{1,9},{2,10},{3,11},{4,12},{5,13},{6,14},{7,15},{8,0},{9,1},... | collective-permute-start | bytes 147464 | tf_op jit(solution)/shard_map/ppermute | solution.py:391
  156.6 6.8 %collective-permute-start.14 = (bf16[48,512]{1,0:T(8,128)(2,1)S(1)}, bf16[48,512]{1,0:T(8,128)(2,1)S(1)}, u32[]{:S(2)}, u32[]{:S(2)}) collective-permute-start(bf16[48,512]{1,0:T(8,128)(2,1)S(1)} %add_convert_fusion.1), channel_id=1, source_target_pairs={{0,4},{1,5},{2,6},{3,7},{4,0},{5,1},{6,2},{7,3},{8,12},{9,13},{10,... | collective-permute-start | bytes 147464 | tf_op jit(solution)/shard_map/ppermute | solution.py:391
  157.6 8.8 %collective-permute-start.10 = (bf16[64,512]{1,0:T(8,128)(2,1)}, bf16[64,512]{1,0:T(8,128)(2,1)S(1)}, u32[]{:S(2)}, u32[]{:S(2)}) collective-permute-start(bf16[64,512]{1,0:T(8,128)(2,1)} %get-tuple-element.31), channel_id=1, source_target_pairs={{0,1},{1,2},{2,3},{3,4},{4,5},{5,6},{6,7},{7,8},{8,9},{9,10},{10,1... | collective-permute-start | bytes 196616 | tf_op jit(solution)/shard_map/ppermute | solution.py:387
  163.4 5.0 %copy-start.1 = (bf16[48,512]{1,0:T(8,128)(2,1)}, bf16[48,512]{1,0:T(8,128)(2,1)S(1)}, u32[]{:S(2)}) copy-start(bf16[48,512]{1,0:T(8,128)(2,1)S(1)} %add_convert_fusion.refs_3_) | copy-start | bytes 147460
  163.5 5.0 %collective-permute-start.17 = (bf16[48,512]{1,0:T(8,128)(2,1)S(1)}, bf16[48,512]{1,0:T(8,128)(2,1)S(1)}, u32[]{:S(2)}, u32[]{:S(2)}) collective-permute-start(bf16[48,512]{1,0:T(8,128)(2,1)S(1)} %add_convert_fusion.refs_3_), channel_id=1, source_target_pairs={{0,16},{1,17},{2,18},{3,19},{4,20},{5,21},{6,22},{7,23},{8,24},{9,... | collective-permute-start | bytes 147464 | tf_op jit(solution)/shard_map/ppermute | solution.py:391
  166.4 2.1 %copy-start.5 = (bf16[64,512]{1,0:T(8,128)(2,1)}, bf16[64,512]{1,0:T(8,128)(2,1)S(1)}, u32[]{:S(2)}) copy-start(bf16[64,512]{1,0:T(8,128)(2,1)S(1)} %collective-permute-done.10.refs_1_) | copy-start | bytes 196612
  168.5 0.6 copy-start.6
where the time goes:
time: 197 us; the launch traced here: 193 us
  blocking collectives  92.5 us (47%)
  starting transfers between devices  38.6 us (20%)
  Pallas kernels  38.6 us (20%)
  waiting for transfers between devices  15.2 us (8%)
  other arithmetic  3.82 us (2%)
  local copies, waits for them, and re-layouts  3.32 us (2%)
    all_to_all x4, blocking collectives, exchange(): return lax.all_to_all(blocks, 'scan', 0, 0, tiled=True)  92.5 us
    ppermute x15, starting transfers between devices, swapped(): return lax.ppermute(block, 'tile', [(i, i ^ bits) for i in range(NT)])  22.8 us
    pallas_call x2, Pallas kernels, patterns(): pl.pallas_call(functools.partial(pattern_kernel, first), out_shape=out, i...  16.4 us
    pallas_call x2, Pallas kernels, illumination(): pl.pallas_call(functools.partial(illum_kernel, last), out_shape=jax.Shape...  10.4 us
    ppermute x15, waiting for transfers between devices, swapped(): return lax.ppermute(block, 'tile', [(i, i ^ bits) for i in range(NT)])  9.94 us
    ppermute x2, starting transfers between devices, shifted(): lax.ppermute(block, 'tile', [(i, i + distance) for i in range(NT) if 0 <=...  9.15 us
    ppermute x1, starting transfers between devices, on_device(): lax.ppermute(outer, 'tile', [(i, i + 1 if i % 2 else i - 1) for i in rang...  6.6 us
    ppermute x2, waiting for transfers between devices, shifted(): lax.ppermute(block, 'tile', [(i, i + distance) for i in range(NT) if 0 <=...  5.21 us
  transfers between devices with their start and end apart: 18, of which 5 were waited for; matrix products, arithmetic and copies ran while one was open for 2% of the time, Pallas kernels for 5%

commit v1 on v0

v1 whole, which is shorter than its diff:
```python
import functools
import math

import jax
import jax.numpy as jnp
import numpy as np
from jax import lax
from jax.experimental import pallas as pl
from jax.experimental.pallas import tpu as pltpu
from jax.sharding import PartitionSpec as P

ITERS = 2
PS = 256
TH = 256
OW = 512
CAP = 12
NS = 8
NT = 32
SR = TH // NS
LN = 128
PAIR = 3
FLOOR2 = 0.25
REG = 1.0

OWN, NEXT, PRB, POS = 0, 2 * SR, 4 * SR, 4 * SR + 48
SEND = POS + 16
GROUP = 12

BF = jnp.bfloat16
F32 = jnp.float32


def tables():
    n = np.arange(PS, dtype=np.int64)
    angle = ((n[:, None] * n[None, :]) % PS).astype(np.float32) * np.float32(2.0 * math.pi / PS)
    c = (np.cos(angle) / np.sqrt(PS)).astype(np.float32)
    s = (np.sin(angle) / np.sqrt(PS)).astype(np.float32)
    return c, s


def table_arrays():
    c, s = tables()
    return [jnp.asarray(np.block(m).astype(jnp.bfloat16)) for m in ([[c, -s], [s, c]], [[c, s], [-s, c]])]


def pattern_kernel(first, pos_ref, cnt_ref, obj_ref, halo_ref, probe_ref, m1_ref, m2_ref, amp_ref, extra_ref, *rest):
    if first:
        send_ref, x, pr, g, pg, patch, h, h2, amp, m1, m2, low, send, extra, sems, amp_sems, out_sems = rest
    else:
        send_ref, objn_ref, probn_ref, x, pr, g, pg, patch, h, h2, amp, m1, m2, low, send, extra, sems, amp_sems, out_sems = rest
    count = cnt_ref[0]
    lane_blocks = [slice(q * LN, (q + 1) * LN) for q in range(4)]
    ins = [(extra_ref, extra), (probe_ref, pr), (halo_ref, low)]
    ins += [(obj_ref.at[k, :, lane_blocks[q]], x.at[k, q, pl.ds(0, TH), :]) for k in range(2) for q in range(4)]
    ins += [(m1_ref, m1), (m2_ref, m2)]
    ins = [pltpu.make_async_copy(src, dst, sems.at[n]) for n, (src, dst) in enumerate(ins)]
    for copy in ins:
        copy.start()

    def amp_copy(j):
        return pltpu.make_async_copy(amp_ref.at[j], amp.at[j], amp_sems.at[j])

    for j in range(PAIR):
        amp_copy(j).start()
    tile_start = lax.axis_index("tile") * TH
    g[...] = jnp.zeros_like(g)
    pg[...] = jnp.zeros_like(pg)
    for copy in ins[:-2]:
        copy.wait()
    outs = []
    if first:
        for q in range(4):
            x[:, q, TH:, :] = low[:, :, lane_blocks[q]].astype(F32)
    else:
        for s in range(NS):
            for k in range(2):
                a = s * SR
                d = extra[s, k * SR : (k + 1) * SR, :].astype(F32)
                e = low[k, a : a + SR, :].astype(F32) + extra[s, (2 + k) * SR : (3 + k) * SR, :].astype(F32)
                for q in range(4):
                    x[k, q, a : a + SR, :] += d[:, lane_blocks[q]]
                    x[k, q, TH + a : TH + a + SR, :] = e[:, lane_blocks[q]]
                d = extra[s, 4 * SR + 16 * k : 4 * SR + 16 * (k + 1), :].astype(F32)
                for q in range(2):
                    b = a + 16 * q
                    pr[k, b : b + 16, :] += d[:, q * PS : (q + 1) * PS]
        outs += [(x.at[k, q, pl.ds(0, TH), :], objn_ref.at[k, :, lane_blocks[q]]) for k in range(2) for q in range(4)]
        outs += [(pr, probn_ref)]
    outs = [pltpu.make_async_copy(src, dst, out_sems.at[n]) for n, (src, dst) in enumerate(outs)]
    for copy in outs:
        copy.start()

    def place(j):
        r = pos_ref[0, j] - tile_start
        c = pos_ref[1, j]
        base = jnp.where(c >= LN, 1, 0)
        return r, base, c - base * LN

    lanes = lax.broadcasted_iota(jnp.int32, (PS, LN), 1)

    def to_half(j, slot, live):
        r, base, off = place(j)
        head = lanes < LN - off
        turn = (LN - off) & (LN - 1)
        xs = []
        for k in range(2):
            v = [pltpu.roll(x[k, base + q, pl.ds(r, PS), :], turn, 1) for q in range(3)]
            v = jnp.concatenate([jnp.where(head, v[0], v[1]), jnp.where(head, v[1], v[2])], 1)
            patch[slot, k] = v
            xs.append(v)
        xr, xi = xs
        p0, p1 = pr[0], pr[1]
        pg[2] += (xr * xr + xi * xi) * live
        w = jnp.concatenate([(p0 * xr - p1 * xi).astype(BF), (p0 * xi + p1 * xr).astype(BF)], 1)
        half = jnp.dot(w, m1[...], preferred_element_type=F32).astype(BF)
        h[slot, :PS, :] = half[:, :PS]
        h[slot, PS:, :] = half[:, PS:]

    def to_back_half(j, slot, live):
        far = jnp.dot(m2[...], h[slot], preferred_element_type=F32)
        fr, fi = far[:PS], far[PS:]
        m = jnp.maximum(fr * fr + fi * fi, FLOOR2)
        q = amp[j].astype(F32) * lax.rsqrt(m) - 1.0
        q = q * live
        u = jnp.concatenate([(q * fr).astype(BF), (q * fi).astype(BF)], 1)
        half = jnp.dot(u, m2[...], preferred_element_type=F32).astype(BF)
        h2[slot, :PS, :] = half[:, :PS]
        h2[slot, PS:, :] = half[:, PS:]

    def add_back(j, slot):
        back = jnp.dot(m1[...], h2[slot], preferred_element_type=F32)
        br, bi = back[:PS], back[PS:]
        xr, xi = patch[slot, 0], patch[slot, 1]
        pg[0] += xr * br + xi * bi
        pg[1] += xr * bi - xi * br
        p0, p1 = pr[0], pr[1]
        r, base, off = place(j)
        tail = lanes >= off
        turn = off & (LN - 1)
        for k, o in enumerate((p0 * br + p1 * bi, p0 * bi - p1 * br)):
            v = [pltpu.roll(o[:, q * LN : (q + 1) * LN], turn, 1) for q in range(2)]
            g[k, base, pl.ds(r, PS), :] += jnp.where(tail, v[0], 0.0)
            g[k, base + 1, pl.ds(r, PS), :] += jnp.where(tail, v[1], v[0])
            g[k, base + 2, pl.ds(r, PS), :] += jnp.where(tail, 0.0, v[1])

    for copy in ins[-2:]:
        copy.wait()

    def visit(i, carry):
        j = [PAIR * i + n for n in range(PAIR)]
        live = [jnp.where(n < count, 1.0, 0.0) for n in j]
        for n in range(PAIR):
            amp_copy(j[n]).wait()

        @pl.when(i + 1 < visits)
        def _():
            for n in range(PAIR):
                amp_copy(j[n] + PAIR).start()

        for n in range(PAIR):
            to_half(j[n], n, live[n])
        for n in range(PAIR):
            to_back_half(j[n], n, live[n])
        for n in range(PAIR):
            add_back(j[n], n)
        return carry

    visits = jnp.clip((count + PAIR - 1) // PAIR, 1, CAP // PAIR)
    lax.fori_loop(0, visits, visit, 0)
    for s in range(NS):
        a = s * SR
        for k in range(2):
            for q in range(4):
                send[s, OWN + k * SR : OWN + (k + 1) * SR, lane_blocks[q]] = g[k, q, a : a + SR, :].astype(BF)
                send[s, NEXT + k * SR : NEXT + (k + 1) * SR, lane_blocks[q]] = g[k, q, TH + a : TH + a + SR, :].astype(BF)
        for k in range(3):
            send[s, PRB + 16 * k : PRB + 16 * (k + 1), :] = jnp.concatenate(
                [pg[k, a : a + 16, :], pg[k, a + 16 : a + 32, :]], 1
            ).astype(BF)
        if first:
            send[s, POS:, :] = extra[...]
        copy = pltpu.make_async_copy(send.at[s], send_ref.at[s], out_sems.at[len(outs)])
        copy.start()
        outs.append(copy)
    for copy in outs:
        copy.wait()


def smem():
    return pl.BlockSpec(memory_space=pltpu.SMEM)


def vmem():
    return pl.BlockSpec(memory_space=pltpu.VMEM)


def anywhere():
    return pl.BlockSpec(memory_space=pl.ANY)


def params(mib):
    return pltpu.CompilerParams(vmem_limit_bytes=mib * 1024 * 1024)


def patterns(pos, cnt, obj, halo, probe, amps, tabs, posblk=None, recv=None):
    first = recv is None
    rows = SEND if first else POS
    out = [jax.ShapeDtypeStruct((NS, rows, OW), BF)]
    if not first:
        out += [jax.ShapeDtypeStruct((2, TH, OW), F32), jax.ShapeDtypeStruct((2, PS, PS), F32)]
    extra = posblk if first else recv
    args = [pos, cnt, obj, halo, probe, *tabs, amps, extra]
    return pl.pallas_call(
        functools.partial(pattern_kernel, first),
        out_shape=out,
        in_specs=[smem(), smem()] + [anywhere()] * (len(args) - 2),
        out_specs=[anywhere()] * len(out),
        scratch_shapes=[
            pltpu.VMEM((2, 4, 2 * TH, LN), F32),
            pltpu.VMEM((2, PS, PS), F32),
            pltpu.VMEM((2, 4, 2 * TH, LN), F32),
            pltpu.VMEM((3, PS, PS), F32),
            pltpu.VMEM((PAIR, 2, PS, PS), F32),
            pltpu.VMEM((PAIR, 2 * PS, PS), BF),
            pltpu.VMEM((PAIR, 2 * PS, PS), BF),
            pltpu.VMEM((CAP, PS, PS), BF),
            pltpu.VMEM((2 * PS, 2 * PS), BF),
            pltpu.VMEM((2 * PS, 2 * PS), BF),
            pltpu.VMEM((2, TH, OW), BF),
            pltpu.VMEM((NS, rows, OW), BF),
            pltpu.VMEM(extra.shape, BF),
            pltpu.SemaphoreType.DMA((13,)),
            pltpu.SemaphoreType.DMA((CAP,)),
            pltpu.SemaphoreType.DMA((9 + NS,)),
        ],
        compiler_params=params(48),
        name="patterns",
    )(*args)


def sum_kernel(last, recv_ref, own_ref, probe_ref, up_ref, *rest):
    *pos_ref, recv, sems = rest
    copies = [pltpu.make_async_copy(recv_ref.at[s], recv.at[s], sems.at[s]) for s in range(NS)]
    for copy in copies:
        copy.start()
    for copy in copies:
        copy.wait()

    def total(a, n):
        t = [recv[s, a : a + n, :].astype(F32) for s in range(NS)]
        return ((t[0] + t[1]) + (t[2] + t[3])) + ((t[4] + t[5]) + (t[6] + t[7]))

    probe_ref[...] = total(PRB, 48).astype(BF)
    own_ref[...] = total(OWN, 2 * SR)
    up_ref[: 2 * SR, :] = total(NEXT, 2 * SR).astype(BF)
    if not last:
        pos = total(POS, 16)
        pos_ref[0][...] = pos[:, :LN]
        up_ref[2 * SR :, :] = pos.astype(BF)


def sums(last, recv):
    out = [jax.ShapeDtypeStruct((2 * SR, OW), F32), jax.ShapeDtypeStruct((48, OW), BF)]
    if last:
        out += [jax.ShapeDtypeStruct((2 * SR, OW), BF)]
    else:
        out += [jax.ShapeDtypeStruct((2 * SR + 16, OW), BF), jax.ShapeDtypeStruct((16, LN), F32)]
    return pl.pallas_call(
        functools.partial(sum_kernel, last),
        out_shape=out,
        in_specs=[anywhere()],
        out_specs=[vmem()] * len(out),
        scratch_shapes=[pltpu.VMEM(recv.shape, BF), pltpu.SemaphoreType.DMA((NS,))],
        compiler_params=params(8),
        name="sums",
    )(recv)


def own_kernel(pos_ref, probe_ref, own_ref, up_ref, out_ref, p2):
    for q in range(2):
        cols = slice(q * LN, (q + 1) * LN)
        p2[q, :SR, :] = jnp.zeros((SR, LN), F32)
        p2[q, SR + PS :, :] = jnp.zeros((SR, LN), F32)
        p2[q, SR : SR + PS, :] = probe_ref[0, :, cols] * probe_ref[0, :, cols] + probe_ref[1, :, cols] * probe_ref[1, :, cols]
    mine = lax.axis_index("scan") * SR
    lanes = lax.broadcasted_iota(jnp.int32, (8, LN), 1)
    parts = SR // 8

    def group(row, carry):
        shift = jnp.where(row < NS, -TH, 0) - 1

        def some(i, carry):
            carry = [list(c) for c in carry]
            for n in range(4):
                code = pos_ref[row, 4 * i + n]
                start = jnp.where(code > 0, code + shift, -4 * TH)
                c = pos_ref[row, GROUP + 4 * i + n]
                far = c >= LN
                off = jnp.where(far, c - LN, c)
                tail = lanes >= off
                turn = off & (LN - 1)
                at = jnp.clip(mine - start, -SR, PS) + SR
                for b in range(parts):
                    y0, y1 = (pltpu.roll(p2[q, pl.ds(at + 8 * b, 8), :], turn, 1) for q in range(2))
                    v = (0.0, jnp.where(tail, y0, 0.0), jnp.where(tail, y1, y0), jnp.where(tail, 0.0, y1), 0.0)
                    for q in range(4):
                        carry[b][q] = carry[b][q] + jnp.where(far, v[q], v[q + 1])
            return tuple(tuple(c) for c in carry)

        return lax.fori_loop(0, (pos_ref[row, 2 * GROUP] + 3) // 4, some, carry)

    zero = jnp.zeros((8, LN), F32)
    carry = lax.fori_loop(0, 2 * NS, group, ((zero,) * 4,) * parts)
    for q in range(4):
        cols = slice(q * LN, (q + 1) * LN)
        scale = 1.0 / (jnp.concatenate([carry[b][q] for b in range(parts)], 0) + REG)
        for k in range(2):
            a = k * SR
            out_ref[a : a + SR, cols] = ((own_ref[a : a + SR, cols] + up_ref[a : a + SR, cols].astype(F32)) * scale).astype(BF)


def own_step(pos, probe, own, up):
    return pl.pallas_call(
        own_kernel,
        out_shape=jax.ShapeDtypeStruct((2 * SR, OW), BF),
        in_specs=[smem(), vmem(), vmem(), vmem()],
        out_specs=vmem(),
        scratch_shapes=[pltpu.VMEM((2, PS + 2 * SR, LN), F32)],
        compiler_params=params(8),
        name="own_step",
    )(pos, probe, own, up)


def spread_kernel(last, *refs):
    *deltas, p0_ref, p1_ref, out_ref, block, sems = refs
    probe = p0_ref[...].astype(F32) + p1_ref[...].astype(F32)
    w = probe[32:] + REG
    at = 0
    for delta in deltas:
        block[at : at + 2 * SR, :] = delta[...]
        at += 2 * SR
    if last:
        root = jnp.sqrt(w)
        parts = [probe[:16] / root, probe[16:32] / root, root]
    else:
        parts = [probe[:16] / w, probe[16:32] / w]
    for part in parts:
        block[at : at + 16, :] = part.astype(BF)
        at += 16
    copies = [pltpu.make_async_copy(block, out_ref.at[s], sems.at[s]) for s in range(NS)]
    for copy in copies:
        copy.start()
    for copy in copies:
        copy.wait()


def spread(last, *args):
    rows = 2 * SR + 48 if last else 4 * SR + 32
    return pl.pallas_call(
        functools.partial(spread_kernel, last),
        out_shape=jax.ShapeDtypeStruct((NS, rows, OW), BF),
        in_specs=[vmem()] * len(args),
        out_specs=anywhere(),
        scratch_shapes=[pltpu.VMEM((rows, OW), BF), pltpu.SemaphoreType.DMA((NS,))],
        compiler_params=params(8),
        name="spread",
    )(*args)


def final_kernel(obj_ref, probe_ref, recv_ref, obj_out, probe_out, grad_out, obj, probe, recv, grad, sems, out_sems):
    ins = []
    for s in range(NS):
        rows = pl.ds(s * SR, SR)
        pairs = [(recv_ref.at[s], recv.at[s]), (obj_ref.at[:, rows, :], obj.at[:, rows, :])]
        pairs += [(probe_ref.at[:, rows, :], probe.at[:, rows, :])]
        ins.append([pltpu.make_async_copy(src, dst, sems.at[s, n]) for n, (src, dst) in enumerate(pairs)])
    for copies in ins:
        for copy in copies:
            copy.start()
    outs = []
    for s in range(NS):
        for copy in ins[s]:
            copy.wait()
        a = s * SR
        root = recv[s, 2 * SR + 32 : 2 * SR + 48, :].astype(F32)
        for k in range(2):
            obj[k, a : a + SR, :] += recv[s, k * SR : (k + 1) * SR, :].astype(F32)
            top = recv[s, 2 * SR + 16 * k : 2 * SR + 16 * (k + 1), :].astype(F32)
            d = top / root
            for q in range(2):
                b = a + 16 * q
                grad[k, b : b + 16, :] = top[:, q * PS : (q + 1) * PS]
                probe[k, b : b + 16, :] += d[:, q * PS : (q + 1) * PS]
        rows = pl.ds(a, SR)
        pairs = [(obj, obj_out), (probe, probe_out), (grad, grad_out)]
        for n, (src, dst) in enumerate(pairs):
            copy = pltpu.make_async_copy(src.at[:, rows, :], dst.at[:, rows, :], out_sems.at[s, n])
            copy.start()
            outs.append(copy)
    for copy in outs:
        copy.wait()


def final(obj, probe, recv):
    return pl.pallas_call(
        final_kernel,
        out_shape=[
            jax.ShapeDtypeStruct((2, TH, OW), F32),
            jax.ShapeDtypeStruct((2, PS, PS), F32),
            jax.ShapeDtypeStruct((2, PS, PS), F32),
        ],
        in_specs=[anywhere()] * 3,
        out_specs=[anywhere()] * 3,
        scratch_shapes=[
            pltpu.VMEM((2, TH, OW), F32),
            pltpu.VMEM((2, PS, PS), F32),
            pltpu.VMEM(recv.shape, BF),
            pltpu.VMEM((2, PS, PS), F32),
            pltpu.SemaphoreType.DMA((NS, 3)),
            pltpu.SemaphoreType.DMA((NS, 3)),
        ],
        compiler_params=params(16),
        name="final",
    )(obj, probe, recv)


def shifted(block, distance):
    return lax.ppermute(block, "tile", [(i, i + distance) for i in range(NT) if 0 <= i + distance < NT])


def swapped(block, bits):
    return lax.ppermute(block, "tile", [(i, i ^ bits) for i in range(NT)])


def four(x, swaps):
    y = [swap.astype(F32) for swap in swaps]
    return ((x.astype(F32) + y[0]) + (y[1] + y[2])).astype(BF)


def exchange(blocks):
    return lax.all_to_all(blocks, "scan", 0, 0, tiled=True)


def on_device(object_field, probe, amplitudes, positions, counts):
    tabs = table_arrays()
    pos = positions[0, 0].T
    cnt = counts[0, 0].reshape(1)
    amps = amplitudes[0, 0]
    halo = shifted(object_field.astype(BF), -1)
    live = lax.broadcasted_iota(jnp.int32, (CAP,), 0) < cnt
    row = jnp.concatenate([jnp.where(live, pos[0] - lax.axis_index("tile") * TH + 1, 0), pos[1], cnt])
    mine = lax.broadcasted_iota(jnp.int32, (16, 1), 0) == lax.axis_index("scan")
    posblk = jnp.where(mine, row[None, :], 0).astype(BF)
    posblk = jnp.pad(posblk, ((0, 0), (0, OW - row.shape[0])))
    coded = 2 * GROUP + 1
    (send,) = patterns(pos, cnt, object_field, halo, probe, amps, tabs, posblk=posblk)
    own, part, up, tile_pos = sums(False, exchange(send))
    swaps = [swapped(part, 1), swapped(part, 2), swapped(part, 3)]
    up = shifted(up, 1)
    part = four(part, swaps)
    swaps = [swapped(part, 4), swapped(part, 8), swapped(part, 12)]
    around = jnp.concatenate([up[2 * SR :, :coded][:NS].astype(F32), tile_pos[:NS, :coded]], 0).astype(jnp.int32)
    delta = own_step(around, probe, own, up)
    part, delta = lax.optimization_barrier((four(part, swaps), delta))
    other = swapped(part, 16)
    recv = exchange(spread(False, delta, shifted(delta, -1), part, other))
    send, object_field, probe = patterns(pos, cnt, object_field, halo, probe, amps, tabs, recv=recv)
    own, part, up = sums(True, exchange(send))
    swaps = [swapped(part, 1), swapped(part, 2), swapped(part, 3)]
    up = shifted(up, 1)
    part = four(part, swaps)
    swaps = [swapped(part, 4), swapped(part, 8), swapped(part, 12)]
    delta = own_step(around, probe, own, up)
    part, delta = lax.optimization_barrier((four(part, swaps), delta))
    other = swapped(part, 16)
    recv = exchange(spread(True, delta, part, other))
    return tuple(final(object_field, probe, recv))


def solution(mesh):
    in_specs = (
        P(None, "tile", None),
        P(),
        P("scan", "tile", None, None, None),
        P("scan", "tile", None, None),
        P("scan", "tile"),
    )
    out_specs = (P(None, "tile", None), P(), P())
    return jax.shard_map(on_device, mesh=mesh, in_specs=in_specs, out_specs=out_specs, check_vma=False)
```

time: 197 us -> 196 us (level); the launches traced: 193 us -> 196 us
  starting transfers between devices: 38.6 us -> 53.3 us
  Pallas kernels: 38.6 us -> 31.1 us
  blocking collectives: 92.5 us -> 87.4 us
  waiting for transfers between devices: 15.2 us -> 18.3 us
  other arithmetic: 3.82 us -> 1.7 us
    ppermute x2 -> x4, starting transfers between devices: 9.15 us -> 19.9 us  [shifted(): lax.ppermute(block, 'tile', [(i, i + distance) for i in range(NT) if 0 <=...]
    ppermute x15 -> x14, starting transfers between devices: 22.8 us -> 33.5 us  [swapped(): return lax.ppermute(block, 'tile', [(i, i ^ bits) for i in range(NT)])]
    ppermute x1 -> x0, starting transfers between devices: 6.6 us -> none  [on_device(): lax.ppermute(outer, 'tile', [(i, i + 1 if i % 2 else i - 1) for i in rang...]
    pallas_call x4, Pallas kernels: 14.7 us -> 8.7 us  [the longest x2 5.6 us: own_step(): pl.pallas_call(own_kernel, out_shape=jax.ShapeDtypeStruct((2 * SR, OW), B...]
    all_to_all x4, blocking collectives: 92.5 us -> 87.4 us  [exchange(): return lax.all_to_all(blocks, 'scan', 0, 0, tiled=True)]
    ppermute x15 -> x14, waiting for transfers between devices: 9.94 us -> 12.5 us  [swapped(): return lax.ppermute(block, 'tile', [(i, i ^ bits) for i in range(NT)])]
    pallas_call x2, Pallas kernels: 16.4 us -> 14.2 us  [patterns(): pl.pallas_call(functools.partial(pattern_kernel, first), out_shape=out, i...]
    ppermute x2 -> x4, waiting for transfers between devices: 5.21 us -> 5.82 us  [shifted(): lax.ppermute(block, 'tile', [(i, i + distance) for i in range(NT) if 0 <=...]
  transfers between devices with their start and end apart: 18 -> 18, of which waited for: 5 -> 8; matrix products, arithmetic and copies ran while one was open for 2% -> 0% of each run, Pallas kernels for 5% -> 3%
where the time goes in v1:
time: 196 us
  blocking collectives  87.4 us (45%)
  starting transfers between devices  53.3 us (27%)
  Pallas kernels  31.1 us (16%)
  waiting for transfers between devices  18.3 us (9%)
  local copies, waits for them, and re-layouts  2.12 us (1%)
    all_to_all x4, blocking collectives, exchange(): return lax.all_to_all(blocks, 'scan', 0, 0, tiled=True)  87.4 us
    ppermute x14, starting transfers between devices, swapped(): return lax.ppermute(block, 'tile', [(i, i ^ bits) for i in range(NT)])  33.5 us
    ppermute x4, starting transfers between devices, shifted(): lax.ppermute(block, 'tile', [(i, i + distance) for i in range(NT) if 0 <=...  19.9 us
    pallas_call x2, Pallas kernels, patterns(): pl.pallas_call(functools.partial(pattern_kernel, first), out_shape=out, i...  14.2 us
    ppermute x14, waiting for transfers between devices, swapped(): return lax.ppermute(block, 'tile', [(i, i ^ bits) for i in range(NT)])  12.5 us
    ppermute x4, waiting for transfers between devices, shifted(): lax.ppermute(block, 'tile', [(i, i + distance) for i in range(NT) if 0 <=...  5.82 us
    pallas_call x2, Pallas kernels, own_step(): pl.pallas_call(own_kernel, out_shape=jax.ShapeDtypeStruct((2 * SR, OW), B...  5.6 us
    pallas_call x2, Pallas kernels, sums(): pl.pallas_call(functools.partial(sum_kernel, last), out_shape=out, in_spe...  4.37 us
  transfers between devices with their start and end apart: 18, of which 8 were waited for; matrix products, arithmetic and copies ran while one was open for 0% of the time, Pallas kernels for 3%

profile of v1, /device:TPU:8, one launch (start us, length us, event | category | flops | bytes accessed | tf_op | source)
XLA Modules:
  0.0 195.7 jit_solution(18293401485501312592)
XLA Ops:
  0.7 1.4 convert_element_type.74
  2.1 7.1 %collective-permute-start = (bf16[2,256,512]{2,1,0:T(8,128)(2,1)S(1)}, bf16[2,256,512]{2,1,0:T(8,128)(2,1)S(1)}, u32[]{:S(2)}, u32[]{:S(2)}) collective-permute-start(bf16[2,256,512]{2,1,0:T(8,128)(2,1)S(1)} %convert_element_type.74), channel_id=1, source_target_pairs={{1,0},{2,1},{3,2},{4,3},{5,4},{6,5},{7,6},{8,7},{9,8},{10,9},{11,1... | collective-permute-start | bytes 1572872 | tf_op jit(solution)/shard_map/ppermute | solution.py:428
  10.0 5.8 %collective-permute-done.halo_ref = bf16[2,256,512]{2,1,0:T(8,128)(2,1)S(1)} collective-permute-done((bf16[2,256,512]{2,1,0:T(8,128)(2,1)S(1)}, bf16[2,256,512]{2,1,0:T(8,128)(2,1)S(1)}, u32[]{:S(2)}, u32[]{:S(2)}) %collective-permute-start) | collective-permute-done | bytes 524320 | tf_op jit(solution)/shard_map/ppermute | solution.py:428
  15.9 1.0 copy-done.2
  16.9 1.0 copy-done.4
  17.9 7.6 %patterns.2 = bf16[8,192,512]{2,1,0:T(8,128)(2,1)S(1)} custom-call(s32[2,12]{1,0:T(2,128)S(1)} %bitcast.16, s32[1]{0:T(128)} %bitcast.11.cnt_ref, f32[2,256,512]{2,1,0:T(8,128)S(1)} %copy-done, bf16[2,256,512]{2,1,0:T(8,128)(2,1)S(1)} %collective-permute-done.halo_ref, f32[2,256,256]{2,1,0:T(8,128)S(1)} %copy-done.1, bf16[512,512]{1,0:T(8,128)(2,1)S(1)} %copy-done.4, ...), custom_call_target="tpu_custom_call" | custom-call | tf_op jit(solution)/shard_map/patterns/pallas_call | solution.py:213
  25.5 25.5 %all_to_all.20.recv_ref = bf16[8,192,512]{2,1,0:T(8,128)(2,1)S(1)} all-to-all(bf16[8,192,512]{2,1,0:T(8,128)(2,1)S(1)} %patterns.2), channel_id=1, replica_groups=mesh['scan'=8,'tile'=32] {'scan'}, dimensions={0} | all-to-all | bytes 3145728 | tf_op jit(solution)/shard_map/all_to_all | solution.py:441
  51.0 2.3 %sums.2 = (f32[64,512]{1,0:T(8,128)S(1)}, bf16[48,512]{1,0:T(8,128)(2,1)S(1)}, bf16[80,512]{1,0:T(8,128)(2,1)S(1)}, f32[16,128]{1,0:T(8,128)S(1)}) custom-call(bf16[8,192,512]{2,1,0:T(8,128)(2,1)S(1)} %all_to_all.20.recv_ref), custom_call_target="tpu_custom_call" | custom-call | tf_op jit(solution)/shard_map/sums/pallas_call | solution.py:268
  53.4 2.0 %collective-permute-start.2 = (bf16[48,512]{1,0:T(8,128)(2,1)S(1)}, bf16[48,512]{1,0:T(8,128)(2,1)S(1)}, u32[]{:S(2)}, u32[]{:S(2)}) collective-permute-start(bf16[48,512]{1,0:T(8,128)(2,1)S(1)} %get-tuple-element.17), channel_id=1, source_target_pairs={{0,2},{1,3},{2,0},{3,1},{4,6},{5,7},{6,4},{7,5},{8,10},{9,11},{10,... | collective-permute-start | bytes 147464 | tf_op jit(solution)/shard_map/ppermute | solution.py:432
  55.4 2.4 %collective-permute-start.7 = (bf16[80,512]{1,0:T(8,128)(2,1)S(1)}, bf16[80,512]{1,0:T(8,128)(2,1)S(1)}, u32[]{:S(2)}, u32[]{:S(2)}) collective-permute-start(bf16[80,512]{1,0:T(8,128)(2,1)S(1)} %get-tuple-element.18), channel_id=1, source_target_pairs={{0,1},{1,2},{2,3},{3,4},{4,5},{5,6},{6,7},{7,8},{8,9},{9,10},{10,1... | collective-permute-start | bytes 245768 | tf_op jit(solution)/shard_map/ppermute | solution.py:428
  58.0 5.9 %collective-permute-start.6 = (bf16[48,512]{1,0:T(8,128)(2,1)S(1)}, bf16[48,512]{1,0:T(8,128)(2,1)S(1)}, u32[]{:S(2)}, u32[]{:S(2)}) collective-permute-start(bf16[48,512]{1,0:T(8,128)(2,1)S(1)} %add_convert_fusion.3), channel_id=1, source_target_pairs={{0,12},{1,13},{2,14},{3,15},{4,8},{5,9},{6,10},{7,11},{8,4},{9,5},... | collective-permute-start | bytes 147464 | tf_op jit(solution)/shard_map/ppermute | solution.py:432
  63.9 2.2 %collective-permute-start.5 = (bf16[48,512]{1,0:T(8,128)(2,1)S(1)}, bf16[48,512]{1,0:T(8,128)(2,1)S(1)}, u32[]{:S(2)}, u32[]{:S(2)}) collective-permute-start(bf16[48,512]{1,0:T(8,128)(2,1)S(1)} %add_convert_fusion.3), channel_id=1, source_target_pairs={{0,8},{1,9},{2,10},{3,11},{4,12},{5,13},{6,14},{7,15},{8,0},{9,1},... | collective-permute-start | bytes 147464 | tf_op jit(solution)/shard_map/ppermute | solution.py:432
  66.4 2.8 %own_step.2.refs_0_ = bf16[64,512]{1,0:T(8,128)(2,1)S(1)} custom-call(s32[16,25]{1,0:T(8,128)S(1)} %maximum_convert_fusion.pos_ref, f32[2,256,256]{2,1,0:T(8,128)S(1)} %copy-done.1, f32[64,512]{1,0:T(8,128)S(1)} %get-tuple-element.20.own_ref, bf16[80,512]{1,0:T(8,128)(2,1)S(1)} %collective-permute-done.7.up_ref), custom_call_target="tpu_custom_call" | custom-call | tf_op jit(solution)/shard_map/own_step/pallas_call | solution.py:323
  69.2 3.9 %collective-permute-done.5 = bf16[48,512]{1,0:T(8,128)(2,1)S(1)} collective-permute-done((bf16[48,512]{1,0:T(8,128)(2,1)S(1)}, bf16[48,512]{1,0:T(8,128)(2,1)S(1)}, u32[]{:S(2)}, u32[]{:S(2)}) %collective-permute-start.5) | collective-permute-done | bytes 49184 | tf_op jit(solution)/shard_map/ppermute | solution.py:432
  73.1 8.0 %collective-permute-start.8 = (bf16[64,512]{1,0:T(8,128)(2,1)S(1)}, bf16[64,512]{1,0:T(8,128)(2,1)S(1)}, u32[]{:S(2)}, u32[]{:S(2)}) collective-permute-start(bf16[64,512]{1,0:T(8,128)(2,1)S(1)} %own_step.2.refs_0_), channel_id=1, source_target_pairs={{1,0},{2,1},{3,2},{4,3},{5,4},{6,5},{7,6},{8,7},{9,8},{10,9},{11,1... | collective-permute-start | bytes 196616 | tf_op jit(solution)/shard_map/ppermute | solution.py:428
  82.1 3.2 %collective-permute-done.9.refs_3_ = bf16[48,512]{1,0:T(8,128)(2,1)S(1)} collective-permute-done((bf16[48,512]{1,0:T(8,128)(2,1)S(1)}, bf16[48,512]{1,0:T(8,128)(2,1)S(1)}, u32[]{:S(2)}, u32[]{:S(2)}) %collective-permute-start.9) | collective-permute-done | bytes 49184 | tf_op jit(solution)/shard_map/ppermute | solution.py:432
  85.4 1.8 spread.2
  87.2 21.7 %all_to_all.21.extra_ref = bf16[8,160,512]{2,1,0:T(8,128)(2,1)S(1)} all-to-all(bf16[8,160,512]{2,1,0:T(8,128)(2,1)S(1)} %spread.2), channel_id=1, replica_groups=mesh['scan'=8,'tile'=32] {'scan'}, dimensions={0} | all-to-all | bytes 2621440 | tf_op jit(solution)/shard_map/all_to_all | solution.py:441
  108.9 6.6 %patterns.3 = (bf16[8,176,512]{2,1,0:T(8,128)(2,1)}, f32[2,256,512]{2,1,0:T(8,128)S(1)}, f32[2,256,256]{2,1,0:T(8,128)S(1)}) custom-call(s32[2,12]{1,0:T(2,128)S(1)} %bitcast.17, s32[1]{0:T(128)} %bitcast.12.cnt_ref, f32[2,256,512]{2,1,0:T(8,128)S(1)} %copy-done, bf16[2,256,512]{2,1,0:T(8,128)(2,1)S(1)} %collective-permute-done.halo_ref, ...), custom_call_target="tpu_custom_call" | custom-call | tf_op jit(solution)/shard_map/patterns/pallas_call | solution.py:213
  115.5 22.8 %all_to_all.22.recv_ref = bf16[8,176,512]{2,1,0:T(8,128)(2,1)S(1)} all-to-all(bf16[8,176,512]{2,1,0:T(8,128)(2,1)} %get-tuple-element.25), channel_id=1, replica_groups=mesh['scan'=8,'tile'=32] {'scan'}, dimensions={0} | all-to-all | bytes 2883584 | tf_op jit(solution)/shard_map/all_to_all | solution.py:441
  138.3 2.1 %sums.3 = (f32[64,512]{1,0:T(8,128)S(1)}, bf16[48,512]{1,0:T(8,128)(2,1)S(1)}, bf16[64,512]{1,0:T(8,128)(2,1)S(1)}) custom-call(bf16[8,176,512]{2,1,0:T(8,128)(2,1)S(1)} %all_to_all.22.recv_ref), custom_call_target="tpu_custom_call" | custom-call | tf_op jit(solution)/shard_map/sums/pallas_call | solution.py:268
  140.5 1.8 collective-permute-start.11
  142.4 2.4 %collective-permute-start.16 = (bf16[64,512]{1,0:T(8,128)(2,1)S(1)}, bf16[64,512]{1,0:T(8,128)(2,1)S(1)}, u32[]{:S(2)}, u32[]{:S(2)}) collective-permute-start(bf16[64,512]{1,0:T(8,128)(2,1)S(1)} %get-tuple-element.28), channel_id=1, source_target_pairs={{0,1},{1,2},{2,3},{3,4},{4,5},{5,6},{6,7},{7,8},{8,9},{9,10},{10,1... | collective-permute-start | bytes 196616 | tf_op jit(solution)/shard_map/ppermute | solution.py:428
  145.2 4.4 %collective-permute-start.15 = (bf16[48,512]{1,0:T(8,128)(2,1)S(1)}, bf16[48,512]{1,0:T(8,128)(2,1)S(1)}, u32[]{:S(2)}, u32[]{:S(2)}) collective-permute-start(bf16[48,512]{1,0:T(8,128)(2,1)S(1)} %add_convert_fusion.1), channel_id=1, source_target_pairs={{0,12},{1,13},{2,14},{3,15},{4,8},{5,9},{6,10},{7,11},{8,4},{9,5},... | collective-permute-start | bytes 147464 | tf_op jit(solution)/shard_map/ppermute | solution.py:432
  149.5 8.7 %collective-permute-start.14 = (bf16[48,512]{1,0:T(8,128)(2,1)S(1)}, bf16[48,512]{1,0:T(8,128)(2,1)S(1)}, u32[]{:S(2)}, u32[]{:S(2)}) collective-permute-start(bf16[48,512]{1,0:T(8,128)(2,1)S(1)} %add_convert_fusion.1), channel_id=1, source_target_pairs={{0,8},{1,9},{2,10},{3,11},{4,12},{5,13},{6,14},{7,15},{8,0},{9,1},... | collective-permute-start | bytes 147464 | tf_op jit(solution)/shard_map/ppermute | solution.py:432
  158.2 2.8 %own_step.3.refs_0_ = bf16[64,512]{1,0:T(8,128)(2,1)S(1)} custom-call(s32[16,25]{1,0:T(8,128)S(1)} %maximum_convert_fusion.pos_ref, f32[2,256,256]{2,1,0:T(8,128)S(1)} %get-tuple-element.24.probe_ref, f32[64,512]{1,0:T(8,128)S(1)} %get-tuple-element.27.own_ref, bf16[64,512]{1,0:T(8,128)(2,1)S(1)} %collective-permute-done.16.up_ref), custom_call_target="tpu_custom_call" | custom-call | tf_op jit(solution)/shard_map/own_step/pallas_call | solution.py:323
  161.5 2.2 %collective-permute-done.13 = bf16[48,512]{1,0:T(8,128)(2,1)S(1)} collective-permute-done((bf16[48,512]{1,0:T(8,128)(2,1)S(1)}, bf16[48,512]{1,0:T(8,128)(2,1)S(1)}, u32[]{:S(2)}, u32[]{:S(2)}) %collective-permute-start.13) | collective-permute-done | bytes 49184 | tf_op jit(solution)/shard_map/ppermute | solution.py:432
  163.7 7.0 %collective-permute-start.17 = (bf16[48,512]{1,0:T(8,128)(2,1)S(1)}, bf16[48,512]{1,0:T(8,128)(2,1)S(1)}, u32[]{:S(2)}, u32[]{:S(2)}) collective-permute-start(bf16[48,512]{1,0:T(8,128)(2,1)S(1)} %add_convert_fusion.refs_1_), channel_id=1, source_target_pairs={{0,16},{1,17},{2,18},{3,19},{4,20},{5,21},{6,22},{7,23},{8,24},{9,... | collective-permute-start | bytes 147464 | tf_op jit(solution)/shard_map/ppermute | solution.py:432
  170.8 2.1 %collective-permute-done.17.refs_2_ = bf16[48,512]{1,0:T(8,128)(2,1)S(1)} collective-permute-done((bf16[48,512]{1,0:T(8,128)(2,1)S(1)}, bf16[48,512]{1,0:T(8,128)(2,1)S(1)}, u32[]{:S(2)}, u32[]{:S(2)}) %collective-permute-start.17) | collective-permute-done | bytes 49184 | tf_op jit(solution)/shard_map/ppermute | solution.py:432
  172.8 1.3 spread.3
  174.1 17.4 %all_to_all.23.recv_ref = bf16[8,112,512]{2,1,0:T(8,128)(2,1)S(1)} all-to-all(bf16[8,112,512]{2,1,0:T(8,128)(2,1)S(1)} %spread.3), channel_id=1, replica_groups=mesh['scan'=8,'tile'=32] {'scan'}, dimensions={0} | all-to-all | bytes 1835008 | tf_op jit(solution)/shard_map/all_to_all | solution.py:441
  191.6 3.9 %final.1 = (f32[2,256,512]{2,1,0:T(8,128)}, f32[2,256,256]{2,1,0:T(8,128)}, f32[2,256,256]{2,1,0:T(8,128)}) custom-call(f32[2,256,512]{2,1,0:T(8,128)S(1)} %get-tuple-element.23.obj_ref, f32[2,256,256]{2,1,0:T(8,128)S(1)} %get-tuple-element.24.probe_ref, bf16[8,112,512]{2,1,0:T(8,128)(2,1)S(1)} %all_to_all.23.recv_ref), custom_call_target="tpu_custom_call" | custom-call | tf_op jit(solution)/shard_map/final/pallas_call | solution.py:405
  (43 shorter events, 2.8 us)
Async XLA Ops:
  0.6 15.2 %copy-start = (f32[2,256,512]{2,1,0:T(8,128)S(1)}, f32[2,256,512]{2,1,0:T(8,128)}, u32[]{:S(2)}) copy-start(f32[2,256,512]{2,1,0:T(8,128)} %obj_ref.3) | copy-start | bytes 3145732
  0.6 9.2 %copy-start.5 = (s32[1,1,12,2]{2,3,1,0:T(2,128)S(1)}, s32[1,1,12,2]{2,3,1,0:T(2,128)}, u32[]{:S(2)}) copy-start(s32[1,1,12,2]{2,3,1,0:T(2,128)} %param.10) | copy-start | bytes 292
  0.7 15.2 %copy-start.1 = (f32[2,256,256]{2,1,0:T(8,128)S(1)}, f32[2,256,256]{2,1,0:T(8,128)}, u32[]{:S(2)}) copy-start(f32[2,256,256]{2,1,0:T(8,128)} %probe_ref.5) | copy-start | bytes 1572868
  2.1 13.8 %collective-permute-start = (bf16[2,256,512]{2,1,0:T(8,128)(2,1)S(1)}, bf16[2,256,512]{2,1,0:T(8,128)(2,1)S(1)}, u32[]{:S(2)}, u32[]{:S(2)}) collective-permute-start(bf16[2,256,512]{2,1,0:T(8,128)(2,1)S(1)} %convert_element_type.74), channel_id=1, source_target_pairs={{1,0},{2,1},{3,2},{4,3},{5,4},{6,5},{7,6},{8,7},{9,8},{10,9},{11,1... | collective-permute-start | bytes 1572872 | tf_op jit(solution)/shard_map/ppermute | solution.py:428
  15.8 1.0 copy-start.2
  16.9 1.0 copy-start.4
  53.3 4.5 %collective-permute-start.3 = (bf16[48,512]{1,0:T(8,128)(2,1)S(1)}, bf16[48,512]{1,0:T(8,128)(2,1)S(1)}, u32[]{:S(2)}, u32[]{:S(2)}) collective-permute-start(bf16[48,512]{1,0:T(8,128)(2,1)S(1)} %get-tuple-element.17), channel_id=1, source_target_pairs={{0,3},{1,2},{2,1},{3,0},{4,7},{5,6},{6,5},{7,4},{8,11},{9,10},{10,... | collective-permute-start | bytes 147464 | tf_op jit(solution)/shard_map/ppermute | solution.py:432
  53.4 4.6 %collective-permute-start.2 = (bf16[48,512]{1,0:T(8,128)(2,1)S(1)}, bf16[48,512]{1,0:T(8,128)(2,1)S(1)}, u32[]{:S(2)}, u32[]{:S(2)}) collective-permute-start(bf16[48,512]{1,0:T(8,128)(2,1)S(1)} %get-tuple-element.17), channel_id=1, source_target_pairs={{0,2},{1,3},{2,0},{3,1},{4,6},{5,7},{6,4},{7,5},{8,10},{9,11},{10,... | collective-permute-start | bytes 147464 | tf_op jit(solution)/shard_map/ppermute | solution.py:432
  55.4 2.6 %collective-permute-start.1 = (bf16[48,512]{1,0:T(8,128)(2,1)S(1)}, bf16[48,512]{1,0:T(8,128)(2,1)S(1)}, u32[]{:S(2)}, u32[]{:S(2)}) collective-permute-start(bf16[48,512]{1,0:T(8,128)(2,1)S(1)} %get-tuple-element.17), channel_id=1, source_target_pairs={{0,1},{1,0},{2,3},{3,2},{4,5},{5,4},{6,7},{7,6},{8,9},{9,8},{10,11... | collective-permute-start | bytes 147464 | tf_op jit(solution)/shard_map/ppermute | solution.py:432
  55.4 11.0 %collective-permute-start.7 = (bf16[80,512]{1,0:T(8,128)(2,1)S(1)}, bf16[80,512]{1,0:T(8,128)(2,1)S(1)}, u32[]{:S(2)}, u32[]{:S(2)}) collective-permute-start(bf16[80,512]{1,0:T(8,128)(2,1)S(1)} %get-tuple-element.18), channel_id=1, source_target_pairs={{0,1},{1,2},{2,3},{3,4},{4,5},{5,6},{6,7},{7,8},{8,9},{9,10},{10,1... | collective-permute-start | bytes 245768 | tf_op jit(solution)/shard_map/ppermute | solution.py:428
  58.0 11.2 %collective-permute-start.6 = (bf16[48,512]{1,0:T(8,128)(2,1)S(1)}, bf16[48,512]{1,0:T(8,128)(2,1)S(1)}, u32[]{:S(2)}, u32[]{:S(2)}) collective-permute-start(bf16[48,512]{1,0:T(8,128)(2,1)S(1)} %add_convert_fusion.3), channel_id=1, source_target_pairs={{0,12},{1,13},{2,14},{3,15},{4,8},{5,9},{6,10},{7,11},{8,4},{9,5},... | collective-permute-start | bytes 147464 | tf_op jit(solution)/shard_map/ppermute | solution.py:432
  63.9 9.2 %collective-permute-start.5 = (bf16[48,512]{1,0:T(8,128)(2,1)S(1)}, bf16[48,512]{1,0:T(8,128)(2,1)S(1)}, u32[]{:S(2)}, u32[]{:S(2)}) collective-permute-start(bf16[48,512]{1,0:T(8,128)(2,1)S(1)} %add_convert_fusion.3), channel_id=1, source_target_pairs={{0,8},{1,9},{2,10},{3,11},{4,12},{5,13},{6,14},{7,15},{8,0},{9,1},... | collective-permute-start | bytes 147464 | tf_op jit(solution)/shard_map/ppermute | solution.py:432
  66.1 7.0 %collective-permute-start.4 = (bf16[48,512]{1,0:T(8,128)(2,1)S(1)}, bf16[48,512]{1,0:T(8,128)(2,1)S(1)}, u32[]{:S(2)}, u32[]{:S(2)}) collective-permute-start(bf16[48,512]{1,0:T(8,128)(2,1)S(1)} %add_convert_fusion.3), channel_id=1, source_target_pairs={{0,4},{1,5},{2,6},{3,7},{4,0},{5,1},{6,2},{7,3},{8,12},{9,13},{10,... | collective-permute-start | bytes 147464 | tf_op jit(solution)/shard_map/ppermute | solution.py:432
  73.1 12.2 %collective-permute-start.8 = (bf16[64,512]{1,0:T(8,128)(2,1)S(1)}, bf16[64,512]{1,0:T(8,128)(2,1)S(1)}, u32[]{:S(2)}, u32[]{:S(2)}) collective-permute-start(bf16[64,512]{1,0:T(8,128)(2,1)S(1)} %own_step.2.refs_0_), channel_id=1, source_target_pairs={{1,0},{2,1},{3,2},{4,3},{5,4},{6,5},{7,6},{8,7},{9,8},{10,9},{11,1... | collective-permute-start | bytes 196616 | tf_op jit(solution)/shard_map/ppermute | solution.py:428
  81.2 4.2 %collective-permute-start.9 = (bf16[48,512]{1,0:T(8,128)(2,1)S(1)}, bf16[48,512]{1,0:T(8,128)(2,1)S(1)}, u32[]{:S(2)}, u32[]{:S(2)}) collective-permute-start(bf16[48,512]{1,0:T(8,128)(2,1)S(1)} %add_convert_fusion.2.refs_2_), channel_id=1, source_target_pairs={{0,16},{1,17},{2,18},{3,19},{4,20},{5,21},{6,22},{7,23},{8,24},{9,... | collective-permute-start | bytes 147464 | tf_op jit(solution)/shard_map/ppermute | solution.py:432
  87.2 21.8 %copy-start.3 = (bf16[512,512]{1,0:T(8,128)(2,1)S(1)}, bf16[512,512]{1,0:T(8,128)(2,1)}, u32[]{:S(2)}) copy-start(bf16[512,512]{1,0:T(8,128)(2,1)} %constant.22.clone.m2_ref) | copy-start | bytes 1572868
  140.4 4.3 %collective-permute-start.12 = (bf16[48,512]{1,0:T(8,128)(2,1)S(1)}, bf16[48,512]{1,0:T(8,128)(2,1)S(1)}, u32[]{:S(2)}, u32[]{:S(2)}) collective-permute-start(bf16[48,512]{1,0:T(8,128)(2,1)S(1)} %get-tuple-element.26), channel_id=1, source_target_pairs={{0,3},{1,2},{2,1},{3,0},{4,7},{5,6},{6,5},{7,4},{8,11},{9,10},{10,... | collective-permute-start | bytes 147464 | tf_op jit(solution)/shard_map/ppermute | solution.py:432
  140.5 4.6 %collective-permute-start.11 = (bf16[48,512]{1,0:T(8,128)(2,1)S(1)}, bf16[48,512]{1,0:T(8,128)(2,1)S(1)}, u32[]{:S(2)}, u32[]{:S(2)}) collective-permute-start(bf16[48,512]{1,0:T(8,128)(2,1)S(1)} %get-tuple-element.26), channel_id=1, source_target_pairs={{0,2},{1,3},{2,0},{3,1},{4,6},{5,7},{6,4},{7,5},{8,10},{9,11},{10,... | collective-permute-start | bytes 147464 | tf_op jit(solution)/shard_map/ppermute | solution.py:432
  142.3 2.8 %collective-permute-start.10 = (bf16[48,512]{1,0:T(8,128)(2,1)S(1)}, bf16[48,512]{1,0:T(8,128)(2,1)S(1)}, u32[]{:S(2)}, u32[]{:S(2)}) collective-permute-start(bf16[48,512]{1,0:T(8,128)(2,1)S(1)} %get-tuple-element.26), channel_id=1, source_target_pairs={{0,1},{1,0},{2,3},{3,2},{4,5},{5,4},{6,7},{7,6},{8,9},{9,8},{10,11... | collective-permute-start | bytes 147464 | tf_op jit(solution)/shard_map/ppermute | solution.py:432
  142.4 15.8 %collective-permute-start.16 = (bf16[64,512]{1,0:T(8,128)(2,1)S(1)}, bf16[64,512]{1,0:T(8,128)(2,1)S(1)}, u32[]{:S(2)}, u32[]{:S(2)}) collective-permute-start(bf16[64,512]{1,0:T(8,128)(2,1)S(1)} %get-tuple-element.28), channel_id=1, source_target_pairs={{0,1},{1,2},{2,3},{3,4},{4,5},{5,6},{6,7},{7,8},{8,9},{9,10},{10,1... | collective-permute-start | bytes 196616 | tf_op jit(solution)/shard_map/ppermute | solution.py:428
  145.2 15.9 %collective-permute-start.15 = (bf16[48,512]{1,0:T(8,128)(2,1)S(1)}, bf16[48,512]{1,0:T(8,128)(2,1)S(1)}, u32[]{:S(2)}, u32[]{:S(2)}) collective-permute-start(bf16[48,512]{1,0:T(8,128)(2,1)S(1)} %add_convert_fusion.1), channel_id=1, source_target_pairs={{0,12},{1,13},{2,14},{3,15},{4,8},{5,9},{6,10},{7,11},{8,4},{9,5},... | collective-permute-start | bytes 147464 | tf_op jit(solution)/shard_map/ppermute | solution.py:432
  149.5 12.0 %collective-permute-start.14 = (bf16[48,512]{1,0:T(8,128)(2,1)S(1)}, bf16[48,512]{1,0:T(8,128)(2,1)S(1)}, u32[]{:S(2)}, u32[]{:S(2)}) collective-permute-start(bf16[48,512]{1,0:T(8,128)(2,1)S(1)} %add_convert_fusion.1), channel_id=1, source_target_pairs={{0,8},{1,9},{2,10},{3,11},{4,12},{5,13},{6,14},{7,15},{8,0},{9,1},... | collective-permute-start | bytes 147464 | tf_op jit(solution)/shard_map/ppermute | solution.py:432
  158.2 5.5 %collective-permute-start.13 = (bf16[48,512]{1,0:T(8,128)(2,1)S(1)}, bf16[48,512]{1,0:T(8,128)(2,1)S(1)}, u32[]{:S(2)}, u32[]{:S(2)}) collective-permute-start(bf16[48,512]{1,0:T(8,128)(2,1)S(1)} %add_convert_fusion.1), channel_id=1, source_target_pairs={{0,4},{1,5},{2,6},{3,7},{4,0},{5,1},{6,2},{7,3},{8,12},{9,13},{10,... | collective-permute-start | bytes 147464 | tf_op jit(solution)/shard_map/ppermute | solution.py:432
  163.7 9.1 %collective-permute-start.17 = (bf16[48,512]{1,0:T(8,128)(2,1)S(1)}, bf16[48,512]{1,0:T(8,128)(2,1)S(1)}, u32[]{:S(2)}, u32[]{:S(2)}) collective-permute-start(bf16[48,512]{1,0:T(8,128)(2,1)S(1)} %add_convert_fusion.refs_1_), channel_id=1, source_target_pairs={{0,16},{1,17},{2,18},{3,19},{4,20},{5,21},{6,22},{7,23},{8,24},{9,... | collective-permute-start | bytes 147464 | tf_op jit(solution)/shard_map/ppermute | solution.py:432

commit v2 on v1

--- a/solution.py
+++ b/solution.py
@@ -18,6 +18,7 @@
 NT = 32
 SR = TH // NS
 LN = 128
+GRANT = 20
 PAIR = 3
 FLOOR2 = 0.25
 REG = 1.0
@@ -43,52 +44,35 @@
     return [jnp.asarray(np.block(m).astype(jnp.bfloat16)) for m in ([[c, -s], [s, c]], [[c, s], [-s, c]])]
 
 
-def pattern_kernel(first, pos_ref, cnt_ref, obj_ref, halo_ref, probe_ref, m1_ref, m2_ref, amp_ref, extra_ref, *rest):
+def pattern_kernel(first, pos_ref, cnt_ref, obj_ref, halo_ref, probe_ref, amp_ref, extra_ref, m1, m2, *rest):
     if first:
-        send_ref, x, pr, g, pg, patch, h, h2, amp, m1, m2, low, send, extra, sems, amp_sems, out_sems = rest
+        send, x, g, pg, patch, h, h2 = rest
+        pr = probe_ref
     else:
-        send_ref, objn_ref, probn_ref, x, pr, g, pg, patch, h, h2, amp, m1, m2, low, send, extra, sems, amp_sems, out_sems = rest
+        send, objn_ref, pr, x, g, pg, patch, h, h2 = rest
     count = cnt_ref[0]
     lane_blocks = [slice(q * LN, (q + 1) * LN) for q in range(4)]
-    ins = [(extra_ref, extra), (probe_ref, pr), (halo_ref, low)]
-    ins += [(obj_ref.at[k, :, lane_blocks[q]], x.at[k, q, pl.ds(0, TH), :]) for k in range(2) for q in range(4)]
-    ins += [(m1_ref, m1), (m2_ref, m2)]
-    ins = [pltpu.make_async_copy(src, dst, sems.at[n]) for n, (src, dst) in enumerate(ins)]
-    for copy in ins:
-        copy.start()
-
-    def amp_copy(j):
-        return pltpu.make_async_copy(amp_ref.at[j], amp.at[j], amp_sems.at[j])
-
-    for j in range(PAIR):
-        amp_copy(j).start()
     tile_start = lax.axis_index("tile") * TH
     g[...] = jnp.zeros_like(g)
     pg[...] = jnp.zeros_like(pg)
-    for copy in ins[:-2]:
-        copy.wait()
-    outs = []
     if first:
         for q in range(4):
-            x[:, q, TH:, :] = low[:, :, lane_blocks[q]].astype(F32)
+            x[:, q, :TH, :] = obj_ref[:, :, lane_blocks[q]]
+            x[:, q, TH:, :] = halo_ref[:, :, lane_blocks[q]].astype(F32)
     else:
         for s in range(NS):
             for k in range(2):
                 a = s * SR
-                d = extra[s, k * SR : (k + 1) * SR, :].astype(F32)
-                e = low[k, a : a + SR, :].astype(F32) + extra[s, (2 + k) * SR : (3 + k) * SR, :].astype(F32)
+                d = obj_ref[k, a : a + SR, :] + extra_ref[s, k * SR : (k + 1) * SR, :].astype(F32)
+                e = halo_ref[k, a : a + SR, :].astype(F32) + extra_ref[s, (2 + k) * SR : (3 + k) * SR, :].astype(F32)
+                objn_ref[k, a : a + SR, :] = d
                 for q in range(4):
-                    x[k, q, a : a + SR, :] += d[:, lane_blocks[q]]
+                    x[k, q, a : a + SR, :] = d[:, lane_blocks[q]]
                     x[k, q, TH + a : TH + a + SR, :] = e[:, lane_blocks[q]]
-                d = extra[s, 4 * SR + 16 * k : 4 * SR + 16 * (k + 1), :].astype(F32)
+                d = extra_ref[s, 4 * SR + 16 * k : 4 * SR + 16 * (k + 1), :].astype(F32)
                 for q in range(2):
                     b = a + 16 * q
-                    pr[k, b : b + 16, :] += d[:, q * PS : (q + 1) * PS]
-        outs += [(x.at[k, q, pl.ds(0, TH), :], objn_ref.at[k, :, lane_blocks[q]]) for k in range(2) for q in range(4)]
-        outs += [(pr, probn_ref)]
-    outs = [pltpu.make_async_copy(src, dst, out_sems.at[n]) for n, (src, dst) in enumerate(outs)]
-    for copy in outs:
-        copy.start()
+                    pr[k, b : b + 16, :] = probe_ref[k, b : b + 16, :] + d[:, q * PS : (q + 1) * PS]
 
     def place(j):
         r = pos_ref[0, j] - tile_start
@@ -120,7 +104,7 @@
         far = jnp.dot(m2[...], h[slot], preferred_element_type=F32)
         fr, fi = far[:PS], far[PS:]
         m = jnp.maximum(fr * fr + fi * fi, FLOOR2)
-        q = amp[j].astype(F32) * lax.rsqrt(m) - 1.0
+        q = amp_ref[j].astype(F32) * lax.rsqrt(m) - 1.0
         q = q * live
         u = jnp.concatenate([(q * fr).astype(BF), (q * fi).astype(BF)], 1)
         half = jnp.dot(u, m2[...], preferred_element_type=F32).astype(BF)
@@ -143,20 +127,9 @@
             g[k, base + 1, pl.ds(r, PS), :] += jnp.where(tail, v[1], v[0])
             g[k, base + 2, pl.ds(r, PS), :] += jnp.where(tail, 0.0, v[1])
 
-    for copy in ins[-2:]:
-        copy.wait()
-
     def visit(i, carry):
         j = [PAIR * i + n for n in range(PAIR)]
         live = [jnp.where(n < count, 1.0, 0.0) for n in j]
-        for n in range(PAIR):
-            amp_copy(j[n]).wait()
-
-        @pl.when(i + 1 < visits)
-        def _():
-            for n in range(PAIR):
-                amp_copy(j[n] + PAIR).start()
-
         for n in range(PAIR):
             to_half(j[n], n, live[n])
         for n in range(PAIR):
@@ -165,8 +138,7 @@
             add_back(j[n], n)
         return carry
 
-    visits = jnp.clip((count + PAIR - 1) // PAIR, 1, CAP // PAIR)
-    lax.fori_loop(0, visits, visit, 0)
+    lax.fori_loop(0, jnp.minimum((count + PAIR - 1) // PAIR, CAP // PAIR), visit, 0)
     for s in range(NS):
         a = s * SR
         for k in range(2):
@@ -178,12 +150,7 @@
                 [pg[k, a : a + 16, :], pg[k, a + 16 : a + 32, :]], 1
             ).astype(BF)
         if first:
-            send[s, POS:, :] = extra[...]
-        copy = pltpu.make_async_copy(send.at[s], send_ref.at[s], out_sems.at[len(outs)])
-        copy.start()
-        outs.append(copy)
-    for copy in outs:
-        copy.wait()
+            send[s, POS:, :] = extra_ref[...]
 
 
 def smem():
@@ -194,60 +161,37 @@
     return pl.BlockSpec(memory_space=pltpu.VMEM)
 
 
-def anywhere():
-    return pl.BlockSpec(memory_space=pl.ANY)
-
-
 def params(mib):
     return pltpu.CompilerParams(vmem_limit_bytes=mib * 1024 * 1024)
 
 
 def patterns(pos, cnt, obj, halo, probe, amps, tabs, posblk=None, recv=None):
     first = recv is None
-    rows = SEND if first else POS
-    out = [jax.ShapeDtypeStruct((NS, rows, OW), BF)]
+    out = [jax.ShapeDtypeStruct((NS, SEND if first else POS, OW), BF)]
     if not first:
         out += [jax.ShapeDtypeStruct((2, TH, OW), F32), jax.ShapeDtypeStruct((2, PS, PS), F32)]
-    extra = posblk if first else recv
-    args = [pos, cnt, obj, halo, probe, *tabs, amps, extra]
+    args = [pos, cnt, obj, halo, probe, amps, posblk if first else recv, *tabs]
     return pl.pallas_call(
         functools.partial(pattern_kernel, first),
         out_shape=out,
-        in_specs=[smem(), smem()] + [anywhere()] * (len(args) - 2),
-        out_specs=[anywhere()] * len(out),
+        in_specs=[smem(), smem()] + [vmem()] * 7,
+        out_specs=[vmem()] * len(out),
         scratch_shapes=[
             pltpu.VMEM((2, 4, 2 * TH, LN), F32),
-            pltpu.VMEM((2, PS, PS), F32),
             pltpu.VMEM((2, 4, 2 * TH, LN), F32),
             pltpu.VMEM((3, PS, PS), F32),
             pltpu.VMEM((PAIR, 2, PS, PS), F32),
             pltpu.VMEM((PAIR, 2 * PS, PS), BF),
             pltpu.VMEM((PAIR, 2 * PS, PS), BF),
-            pltpu.VMEM((CAP, PS, PS), BF),
-            pltpu.VMEM((2 * PS, 2 * PS), BF),
-            pltpu.VMEM((2 * PS, 2 * PS), BF),
-            pltpu.VMEM((2, TH, OW), BF),
-            pltpu.VMEM((NS, rows, OW), BF),
-            pltpu.VMEM(extra.shape, BF),
-            pltpu.SemaphoreType.DMA((13,)),
-            pltpu.SemaphoreType.DMA((CAP,)),
-            pltpu.SemaphoreType.DMA((9 + NS,)),
         ],
-        compiler_params=params(48),
+        compiler_params=params(GRANT),
         name="patterns",
     )(*args)
 
 
 def sum_kernel(last, recv_ref, own_ref, probe_ref, up_ref, *rest):
-    *pos_ref, recv, sems = rest
-    copies = [pltpu.make_async_copy(recv_ref.at[s], recv.at[s], sems.at[s]) for s in range(NS)]
-    for copy in copies:
-        copy.start()
-    for copy in copies:
-        copy.wait()
-
     def total(a, n):
-        t = [recv[s, a : a + n, :].astype(F32) for s in range(NS)]
+        t = [recv_ref[s, a : a + n, :].astype(F32) for s in range(NS)]
         return ((t[0] + t[1]) + (t[2] + t[3])) + ((t[4] + t[5]) + (t[6] + t[7]))
 
     probe_ref[...] = total(PRB, 48).astype(BF)
@@ -255,7 +199,7 @@
     up_ref[: 2 * SR, :] = total(NEXT, 2 * SR).astype(BF)
     if not last:
         pos = total(POS, 16)
-        pos_ref[0][...] = pos[:, :LN]
+        rest[0][...] = pos[:, :LN]
         up_ref[2 * SR :, :] = pos.astype(BF)
 
 
@@ -268,9 +212,8 @@
     return pl.pallas_call(
         functools.partial(sum_kernel, last),
         out_shape=out,
-        in_specs=[anywhere()],
+        in_specs=[vmem()],
         out_specs=[vmem()] * len(out),
-        scratch_shapes=[pltpu.VMEM(recv.shape, BF), pltpu.SemaphoreType.DMA((NS,))],
         compiler_params=params(8),
         name="sums",
     )(recv)
@@ -332,26 +275,21 @@
 
 
 def spread_kernel(last, *refs):
-    *deltas, p0_ref, p1_ref, out_ref, block, sems = refs
+    *deltas, p0_ref, p1_ref, out_ref = refs
     probe = p0_ref[...].astype(F32) + p1_ref[...].astype(F32)
     w = probe[32:] + REG
-    at = 0
-    for delta in deltas:
-        block[at : at + 2 * SR, :] = delta[...]
-        at += 2 * SR
+    parts = [delta[...] for delta in deltas]
     if last:
         root = jnp.sqrt(w)
-        parts = [probe[:16] / root, probe[16:32] / root, root]
+        parts += [probe[:16] / root, probe[16:32] / root, root]
     else:
-        parts = [probe[:16] / w, probe[16:32] / w]
+        parts += [probe[:16] / w, probe[16:32] / w]
+    at = 0
     for part in parts:
-        block[at : at + 16, :] = part.astype(BF)
-        at += 16
-    copies = [pltpu.make_async_copy(block, out_ref.at[s], sems.at[s]) for s in range(NS)]
-    for copy in copies:
-        copy.start()
-    for copy in copies:
-        copy.wait()
+        n = part.shape[0]
+        for s in range(NS):
+            out_ref[s, at : at + n, :] = part.astype(BF)
+        at += n
 
 
 def spread(last, *args):
@@ -360,45 +298,24 @@
         functools.partial(spread_kernel, last),
         out_shape=jax.ShapeDtypeStruct((NS, rows, OW), BF),
         in_specs=[vmem()] * len(args),
-        out_specs=anywhere(),
-        scratch_shapes=[pltpu.VMEM((rows, OW), BF), pltpu.SemaphoreType.DMA((NS,))],
+        out_specs=vmem(),
         compiler_params=params(8),
         name="spread",
     )(*args)
 
 
-def final_kernel(obj_ref, probe_ref, recv_ref, obj_out, probe_out, grad_out, obj, probe, recv, grad, sems, out_sems):
-    ins = []
+def final_kernel(obj_ref, probe_ref, recv_ref, obj_out, probe_out, grad_out):
     for s in range(NS):
-        rows = pl.ds(s * SR, SR)
-        pairs = [(recv_ref.at[s], recv.at[s]), (obj_ref.at[:, rows, :], obj.at[:, rows, :])]
-        pairs += [(probe_ref.at[:, rows, :], probe.at[:, rows, :])]
-        ins.append([pltpu.make_async_copy(src, dst, sems.at[s, n]) for n, (src, dst) in enumerate(pairs)])
-    for copies in ins:
-        for copy in copies:
-            copy.start()
-    outs = []
-    for s in range(NS):
-        for copy in ins[s]:
-            copy.wait()
         a = s * SR
-        root = recv[s, 2 * SR + 32 : 2 * SR + 48, :].astype(F32)
+        root = recv_ref[s, 2 * SR + 32 : 2 * SR + 48, :].astype(F32)
         for k in range(2):
-            obj[k, a : a + SR, :] += recv[s, k * SR : (k + 1) * SR, :].astype(F32)
-            top = recv[s, 2 * SR + 16 * k : 2 * SR + 16 * (k + 1), :].astype(F32)
-            d = top / root
+            obj_out[k, a : a + SR, :] = obj_ref[k, a : a + SR, :] + recv_ref[s, k * SR : (k + 1) * SR, :].astype(F32)
+            grad = recv_ref[s, 2 * SR + 16 * k : 2 * SR + 16 * (k + 1), :].astype(F32)
+            d = grad / root
             for q in range(2):
                 b = a + 16 * q
-                grad[k, b : b + 16, :] = top[:, q * PS : (q + 1) * PS]
-                probe[k, b : b + 16, :] += d[:, q * PS : (q + 1) * PS]
-        rows = pl.ds(a, SR)
-        pairs = [(obj, obj_out), (probe, probe_out), (grad, grad_out)]
-        for n, (src, dst) in enumerate(pairs):
-            copy = pltpu.make_async_copy(src.at[:, rows, :], dst.at[:, rows, :], out_sems.at[s, n])
-            copy.start()
-            outs.append(copy)
-    for copy in outs:
-        copy.wait()
+                grad_out[k, b : b + 16, :] = grad[:, q * PS : (q + 1) * PS]
+                probe_out[k, b : b + 16, :] = probe_ref[k, b : b + 16, :] + d[:, q * PS : (q + 1) * PS]
 
 
 def final(obj, probe, recv):
@@ -409,17 +326,9 @@
             jax.ShapeDtypeStruct((2, PS, PS), F32),
             jax.ShapeDtypeStruct((2, PS, PS), F32),
         ],
-        in_specs=[anywhere()] * 3,
-        out_specs=[anywhere()] * 3,
-        scratch_shapes=[
-            pltpu.VMEM((2, TH, OW), F32),
-            pltpu.VMEM((2, PS, PS), F32),
-            pltpu.VMEM(recv.shape, BF),
-            pltpu.VMEM((2, PS, PS), F32),
-            pltpu.SemaphoreType.DMA((NS, 3)),
-            pltpu.SemaphoreType.DMA((NS, 3)),
-        ],
-        compiler_params=params(16),
+        in_specs=[vmem()] * 3,
+        out_specs=[vmem()] * 3,
+        compiler_params=params(8),
         name="final",
     )(obj, probe, recv)
 

time: 196 us -> 176 us (0.90); the launches traced: 196 us -> 173 us
  Pallas kernels: 31.1 us -> 17.8 us
  blocking collectives: 87.4 us -> 81.2 us
  starting transfers between devices: 53.3 us -> 49.2 us
    all_to_all x4, blocking collectives: 87.4 us -> 81.2 us  [exchange(): return lax.all_to_all(blocks, 'scan', 0, 0, tiled=True)]
    pallas_call x2, Pallas kernels: 14.2 us -> 8.9 us  [patterns(): pl.pallas_call(functools.partial(pattern_kernel, first), out_shape=out, i...]
    pallas_call x2, Pallas kernels: 4.37 us -> 0.38 us  [sums(): pl.pallas_call(functools.partial(sum_kernel, last), out_shape=out, in_spe...]
    ppermute x14, starting transfers between devices: 33.5 us -> 29.7 us  [swapped(): return lax.ppermute(block, 'tile', [(i, i ^ bits) for i in range(NT)])]
    pallas_call x2, Pallas kernels: 3.09 us -> 0.15 us  [spread(): pl.pallas_call(functools.partial(spread_kernel, last), out_shape=jax.Shap...]
    pallas_call x1, Pallas kernels: 3.9 us -> 1.44 us  [final(): pl.pallas_call(final_kernel, out_shape=[jax.ShapeDtypeStruct((2, TH, OW),...]
  transfers between devices with their start and end apart: 18 -> 18, of which waited for: 8 -> 8; matrix products, arithmetic and copies ran while one was open for 0% -> 0% of each run, Pallas kernels for 3% -> 4%
where the time goes in v2:
time: 176 us; the launch traced here: 173 us
  blocking collectives  81.2 us (46%)
  starting transfers between devices  49.2 us (28%)
  waiting for transfers between devices  17.8 us (10%)
  Pallas kernels  17.8 us (10%)
  local copies, waits for them, and re-layouts  3.52 us (2%)
    all_to_all x4, blocking collectives, exchange(): return lax.all_to_all(blocks, 'scan', 0, 0, tiled=True)  81.2 us
    ppermute x14, starting transfers between devices, swapped(): return lax.ppermute(block, 'tile', [(i, i ^ bits) for i in range(NT)])  29.7 us
    ppermute x4, starting transfers between devices, shifted(): lax.ppermute(block, 'tile', [(i, i + distance) for i in range(NT) if 0 <=...  19.4 us
    ppermute x14, waiting for transfers between devices, swapped(): return lax.ppermute(block, 'tile', [(i, i ^ bits) for i in range(NT)])  10.8 us
    pallas_call x2, Pallas kernels, patterns(): pl.pallas_call(functools.partial(pattern_kernel, first), out_shape=out, i...  8.9 us
    ppermute x4, waiting for transfers between devices, shifted(): lax.ppermute(block, 'tile', [(i, i + distance) for i in range(NT) if 0 <=...  6.94 us
    pallas_call x2, Pallas kernels, own_step(): pl.pallas_call(own_kernel, out_shape=jax.ShapeDtypeStruct((2 * SR, OW), B...  6.92 us
  transfers between devices with their start and end apart: 18, of which 8 were waited for; matrix products, arithmetic and copies ran while one was open for 0% of the time, Pallas kernels for 4%

profile of v2, /device:TPU:8, one launch (start us, length us, event | category | flops | bytes accessed | tf_op | source)
XLA Modules:
  0.0 172.7 jit_solution(2876826939637147629)
XLA Ops:
  0.7 1.4 convert_element_type.74
  2.1 7.1 %collective-permute-start = (bf16[2,256,512]{2,1,0:T(8,128)(2,1)S(1)}, bf16[2,256,512]{2,1,0:T(8,128)(2,1)S(1)}, u32[]{:S(2)}, u32[]{:S(2)}) collective-permute-start(bf16[2,256,512]{2,1,0:T(8,128)(2,1)S(1)} %convert_element_type.74), channel_id=1, source_target_pairs={{1,0},{2,1},{3,2},{4,3},{5,4},{6,5},{7,6},{8,7},{9,8},{10,9},{11,1... | collective-permute-start | bytes 1572872 | tf_op jit(solution)/shard_map/ppermute | solution.py:337
  10.0 5.8 %collective-permute-done.halo_ref = bf16[2,256,512]{2,1,0:T(8,128)(2,1)S(1)} collective-permute-done((bf16[2,256,512]{2,1,0:T(8,128)(2,1)S(1)}, bf16[2,256,512]{2,1,0:T(8,128)(2,1)S(1)}, u32[]{:S(2)}, u32[]{:S(2)}) %collective-permute-start) | collective-permute-done | bytes 524320 | tf_op jit(solution)/shard_map/ppermute | solution.py:337
  15.9 1.4 copy-done.1
  17.3 1.0 copy-done.3
  18.3 1.0 copy-done.5
  19.3 4.2 %patterns.2 = bf16[8,192,512]{2,1,0:T(8,128)(2,1)S(1)} custom-call(s32[2,12]{1,0:T(2,128)S(1)} %bitcast.18, s32[1]{0:T(128)} %bitcast.11.cnt_ref, f32[2,256,512]{2,1,0:T(8,128)S(1)} %copy-done, bf16[2,256,512]{2,1,0:T(8,128)(2,1)S(1)} %collective-permute-done.halo_ref, f32[2,256,256]{2,1,0:T(8,128)S(1)} %copy-done.2, bf16[12,256,256]{2,1,0:T(8,128)(2,1)S(1)} %bitcast.14, ...), custom_call_target="tpu_custom_call" | custom-call | tf_op jit(solution)/shard_map/patterns/pallas_call | solution.py:174
  23.6 25.5 %all_to_all.20.recv_ref = bf16[8,192,512]{2,1,0:T(8,128)(2,1)S(1)} all-to-all(bf16[8,192,512]{2,1,0:T(8,128)(2,1)S(1)} %patterns.2), channel_id=1, replica_groups=mesh['scan'=8,'tile'=32] {'scan'}, dimensions={0} | all-to-all | bytes 3145728 | tf_op jit(solution)/shard_map/all_to_all | solution.py:350
  49.3 3.4 %collective-permute-start.3 = (bf16[48,512]{1,0:T(8,128)(2,1)S(1)}, bf16[48,512]{1,0:T(8,128)(2,1)S(1)}, u32[]{:S(2)}, u32[]{:S(2)}) collective-permute-start(bf16[48,512]{1,0:T(8,128)(2,1)S(1)} %get-tuple-element.17), channel_id=1, source_target_pairs={{0,3},{1,2},{2,1},{3,0},{4,7},{5,6},{6,5},{7,4},{8,11},{9,10},{10,... | collective-permute-start | bytes 147464 | tf_op jit(solution)/shard_map/ppermute | solution.py:341
  53.0 2.2 %collective-permute-start.7 = (bf16[80,512]{1,0:T(8,128)(2,1)S(1)}, bf16[80,512]{1,0:T(8,128)(2,1)S(1)}, u32[]{:S(2)}, u32[]{:S(2)}) collective-permute-start(bf16[80,512]{1,0:T(8,128)(2,1)S(1)} %get-tuple-element.18), channel_id=1, source_target_pairs={{0,1},{1,2},{2,3},{3,4},{4,5},{5,6},{6,7},{7,8},{8,9},{9,10},{10,1... | collective-permute-start | bytes 245768 | tf_op jit(solution)/shard_map/ppermute | solution.py:337
  55.2 1.7 collective-permute-done.2
  56.9 3.1 %collective-permute-start.6 = (bf16[48,512]{1,0:T(8,128)(2,1)S(1)}, bf16[48,512]{1,0:T(8,128)(2,1)S(1)}, u32[]{:S(2)}, u32[]{:S(2)}) collective-permute-start(bf16[48,512]{1,0:T(8,128)(2,1)S(1)} %add_convert_fusion.3), channel_id=1, source_target_pairs={{0,12},{1,13},{2,14},{3,15},{4,8},{5,9},{6,10},{7,11},{8,4},{9,5},... | collective-permute-start | bytes 147464 | tf_op jit(solution)/shard_map/ppermute | solution.py:341
  59.9 1.2 collective-permute-start.5
  61.1 2.3 %collective-permute-start.4 = (bf16[48,512]{1,0:T(8,128)(2,1)S(1)}, bf16[48,512]{1,0:T(8,128)(2,1)S(1)}, u32[]{:S(2)}, u32[]{:S(2)}) collective-permute-start(bf16[48,512]{1,0:T(8,128)(2,1)S(1)} %add_convert_fusion.3), channel_id=1, source_target_pairs={{0,4},{1,5},{2,6},{3,7},{4,0},{5,1},{6,2},{7,3},{8,12},{9,13},{10,... | collective-permute-start | bytes 147464 | tf_op jit(solution)/shard_map/ppermute | solution.py:341
  63.4 1.1 collective-permute-done.7.up_ref
  64.6 3.5 %own_step.2.refs_0_ = bf16[64,512]{1,0:T(8,128)(2,1)S(1)} custom-call(s32[16,25]{1,0:T(8,128)S(1)} %maximum_convert_fusion.pos_ref, f32[2,256,256]{2,1,0:T(8,128)S(1)} %copy-done.2, f32[64,512]{1,0:T(8,128)S(1)} %get-tuple-element.20.own_ref, bf16[80,512]{1,0:T(8,128)(2,1)S(1)} %collective-permute-done.7.up_ref), custom_call_target="tpu_custom_call" | custom-call | tf_op jit(solution)/shard_map/own_step/pallas_call | solution.py:266
  68.1 0.5 collective-permute-done.5
  68.6 7.9 %collective-permute-start.8 = (bf16[64,512]{1,0:T(8,128)(2,1)S(1)}, bf16[64,512]{1,0:T(8,128)(2,1)S(1)}, u32[]{:S(2)}, u32[]{:S(2)}) collective-permute-start(bf16[64,512]{1,0:T(8,128)(2,1)S(1)} %own_step.2.refs_0_), channel_id=1, source_target_pairs={{1,0},{2,1},{3,2},{4,3},{5,4},{6,5},{7,6},{8,7},{9,8},{10,9},{11,1... | collective-permute-start | bytes 196616 | tf_op jit(solution)/shard_map/ppermute | solution.py:337
  76.7 4.1 %collective-permute-done.9.refs_3_ = bf16[48,512]{1,0:T(8,128)(2,1)S(1)} collective-permute-done((bf16[48,512]{1,0:T(8,128)(2,1)S(1)}, bf16[48,512]{1,0:T(8,128)(2,1)S(1)}, u32[]{:S(2)}, u32[]{:S(2)}) %collective-permute-start.9) | collective-permute-done | bytes 49184 | tf_op jit(solution)/shard_map/ppermute | solution.py:341
  80.9 19.1 %all_to_all.21.extra_ref = bf16[8,160,512]{2,1,0:T(8,128)(2,1)S(1)} all-to-all(bf16[8,160,512]{2,1,0:T(8,128)(2,1)S(1)} %spread.2), channel_id=1, replica_groups=mesh['scan'=8,'tile'=32] {'scan'}, dimensions={0} | all-to-all | bytes 2621440 | tf_op jit(solution)/shard_map/all_to_all | solution.py:350
  100.0 4.7 %patterns.3 = (bf16[8,176,512]{2,1,0:T(8,128)(2,1)S(1)}, f32[2,256,512]{2,1,0:T(8,128)S(1)}, f32[2,256,256]{2,1,0:T(8,128)S(1)}) custom-call(s32[2,12]{1,0:T(2,128)S(1)} %bitcast.19, s32[1]{0:T(128)} %bitcast.12.cnt_ref, f32[2,256,512]{2,1,0:T(8,128)S(1)} %copy-done, bf16[2,256,512]{2,1,0:T(8,128)(2,1)S(1)} %collective-permute-done.halo_ref, ...), custom_call_target="tpu_custom_call" | custom-call | tf_op jit(solution)/shard_map/patterns/pallas_call | solution.py:174
  104.6 20.6 %all_to_all.22.recv_ref = bf16[8,176,512]{2,1,0:T(8,128)(2,1)S(1)} all-to-all(bf16[8,176,512]{2,1,0:T(8,128)(2,1)S(1)} %get-tuple-element.25), channel_id=1, replica_groups=mesh['scan'=8,'tile'=32] {'scan'}, dimensions={0} | all-to-all | bytes 2883584 | tf_op jit(solution)/shard_map/all_to_all | solution.py:350
  125.4 9.1 %collective-permute-start.12 = (bf16[48,512]{1,0:T(8,128)(2,1)S(1)}, bf16[48,512]{1,0:T(8,128)(2,1)S(1)}, u32[]{:S(2)}, u32[]{:S(2)}) collective-permute-start(bf16[48,512]{1,0:T(8,128)(2,1)S(1)} %get-tuple-element.26), channel_id=1, source_target_pairs={{0,3},{1,2},{2,1},{3,0},{4,7},{5,6},{6,5},{7,4},{8,11},{9,10},{10,... | collective-permute-start | bytes 147464 | tf_op jit(solution)/shard_map/ppermute | solution.py:341
  134.8 2.2 %collective-permute-start.16 = (bf16[64,512]{1,0:T(8,128)(2,1)S(1)}, bf16[64,512]{1,0:T(8,128)(2,1)S(1)}, u32[]{:S(2)}, u32[]{:S(2)}) collective-permute-start(bf16[64,512]{1,0:T(8,128)(2,1)S(1)} %get-tuple-element.28), channel_id=1, source_target_pairs={{0,1},{1,2},{2,3},{3,4},{4,5},{5,6},{6,7},{7,8},{8,9},{9,10},{10,1... | collective-permute-start | bytes 196616 | tf_op jit(solution)/shard_map/ppermute | solution.py:337
  137.0 1.7 collective-permute-done.11
  138.9 6.4 %collective-permute-start.13 = (bf16[48,512]{1,0:T(8,128)(2,1)S(1)}, bf16[48,512]{1,0:T(8,128)(2,1)S(1)}, u32[]{:S(2)}, u32[]{:S(2)}) collective-permute-start(bf16[48,512]{1,0:T(8,128)(2,1)S(1)} %add_convert_fusion.1), channel_id=1, source_target_pairs={{0,4},{1,5},{2,6},{3,7},{4,0},{5,1},{6,2},{7,3},{8,12},{9,13},{10,... | collective-permute-start | bytes 147464 | tf_op jit(solution)/shard_map/ppermute | solution.py:341
  145.3 3.5 %own_step.3.refs_0_ = bf16[64,512]{1,0:T(8,128)(2,1)S(1)} custom-call(s32[16,25]{1,0:T(8,128)S(1)} %maximum_convert_fusion.pos_ref, f32[2,256,256]{2,1,0:T(8,128)S(1)} %get-tuple-element.24.probe_ref, f32[64,512]{1,0:T(8,128)S(1)} %get-tuple-element.27.own_ref, bf16[64,512]{1,0:T(8,128)(2,1)S(1)} %collective-permute-done.16.up_ref), custom_call_target="tpu_custom_call" | custom-call | tf_op jit(solution)/shard_map/own_step/pallas_call | solution.py:266
  148.7 0.8 collective-permute-done.13
  149.6 3.5 %collective-permute-start.17 = (bf16[48,512]{1,0:T(8,128)(2,1)S(1)}, bf16[48,512]{1,0:T(8,128)(2,1)S(1)}, u32[]{:S(2)}, u32[]{:S(2)}) collective-permute-start(bf16[48,512]{1,0:T(8,128)(2,1)S(1)} %add_convert_fusion.refs_1_), channel_id=1, source_target_pairs={{0,16},{1,17},{2,18},{3,19},{4,20},{5,21},{6,22},{7,23},{8,24},{9,... | collective-permute-start | bytes 147464 | tf_op jit(solution)/shard_map/ppermute | solution.py:341
  153.1 2.1 %collective-permute-done.17.refs_2_ = bf16[48,512]{1,0:T(8,128)(2,1)S(1)} collective-permute-done((bf16[48,512]{1,0:T(8,128)(2,1)S(1)}, bf16[48,512]{1,0:T(8,128)(2,1)S(1)}, u32[]{:S(2)}, u32[]{:S(2)}) %collective-permute-start.17) | collective-permute-done | bytes 49184 | tf_op jit(solution)/shard_map/ppermute | solution.py:341
  155.2 16.0 %all_to_all.23.recv_ref = bf16[8,112,512]{2,1,0:T(8,128)(2,1)S(1)} all-to-all(bf16[8,112,512]{2,1,0:T(8,128)(2,1)S(1)} %spread.3), channel_id=1, replica_groups=mesh['scan'=8,'tile'=32] {'scan'}, dimensions={0} | all-to-all | bytes 1835008 | tf_op jit(solution)/shard_map/all_to_all | solution.py:350
  171.2 1.4 final.1
  (45 shorter events, 1.6 us)
Async XLA Ops:
  0.6 15.2 %copy-start = (f32[2,256,512]{2,1,0:T(8,128)S(1)}, f32[2,256,512]{2,1,0:T(8,128)}, u32[]{:S(2)}) copy-start(f32[2,256,512]{2,1,0:T(8,128)} %obj_ref.3) | copy-start | bytes 3145732
  0.6 9.2 %copy-start.6 = (s32[1,1,12,2]{2,3,1,0:T(2,128)S(1)}, s32[1,1,12,2]{2,3,1,0:T(2,128)}, u32[]{:S(2)}) copy-start(s32[1,1,12,2]{2,3,1,0:T(2,128)} %param.10) | copy-start | bytes 292
  0.7 15.2 %copy-start.2 = (f32[2,256,256]{2,1,0:T(8,128)S(1)}, f32[2,256,256]{2,1,0:T(8,128)}, u32[]{:S(2)}) copy-start(f32[2,256,256]{2,1,0:T(8,128)} %probe_ref.5) | copy-start | bytes 1572868
  2.1 13.8 %collective-permute-start = (bf16[2,256,512]{2,1,0:T(8,128)(2,1)S(1)}, bf16[2,256,512]{2,1,0:T(8,128)(2,1)S(1)}, u32[]{:S(2)}, u32[]{:S(2)}) collective-permute-start(bf16[2,256,512]{2,1,0:T(8,128)(2,1)S(1)} %convert_element_type.74), channel_id=1, source_target_pairs={{1,0},{2,1},{3,2},{4,3},{5,4},{6,5},{7,6},{8,7},{9,8},{10,9},{11,1... | collective-permute-start | bytes 1572872 | tf_op jit(solution)/shard_map/ppermute | solution.py:337
  15.8 1.4 copy-start.1
  17.3 1.0 copy-start.3
  18.3 1.0 copy-start.5
  49.3 5.9 %collective-permute-start.3 = (bf16[48,512]{1,0:T(8,128)(2,1)S(1)}, bf16[48,512]{1,0:T(8,128)(2,1)S(1)}, u32[]{:S(2)}, u32[]{:S(2)}) collective-permute-start(bf16[48,512]{1,0:T(8,128)(2,1)S(1)} %get-tuple-element.17), channel_id=1, source_target_pairs={{0,3},{1,2},{2,1},{3,0},{4,7},{5,6},{6,5},{7,4},{8,11},{9,10},{10,... | collective-permute-start | bytes 147464 | tf_op jit(solution)/shard_map/ppermute | solution.py:341
  52.7 4.1 %collective-permute-start.2 = (bf16[48,512]{1,0:T(8,128)(2,1)S(1)}, bf16[48,512]{1,0:T(8,128)(2,1)S(1)}, u32[]{:S(2)}, u32[]{:S(2)}) collective-permute-start(bf16[48,512]{1,0:T(8,128)(2,1)S(1)} %get-tuple-element.17), channel_id=1, source_target_pairs={{0,2},{1,3},{2,0},{3,1},{4,6},{5,7},{6,4},{7,5},{8,10},{9,11},{10,... | collective-permute-start | bytes 147464 | tf_op jit(solution)/shard_map/ppermute | solution.py:341
  52.7 4.1 %collective-permute-start.1 = (bf16[48,512]{1,0:T(8,128)(2,1)S(1)}, bf16[48,512]{1,0:T(8,128)(2,1)S(1)}, u32[]{:S(2)}, u32[]{:S(2)}) collective-permute-start(bf16[48,512]{1,0:T(8,128)(2,1)S(1)} %get-tuple-element.17), channel_id=1, source_target_pairs={{0,1},{1,0},{2,3},{3,2},{4,5},{5,4},{6,7},{7,6},{8,9},{9,8},{10,11... | collective-permute-start | bytes 147464 | tf_op jit(solution)/shard_map/ppermute | solution.py:341
  53.0 11.6 %collective-permute-start.7 = (bf16[80,512]{1,0:T(8,128)(2,1)S(1)}, bf16[80,512]{1,0:T(8,128)(2,1)S(1)}, u32[]{:S(2)}, u32[]{:S(2)}) collective-permute-start(bf16[80,512]{1,0:T(8,128)(2,1)S(1)} %get-tuple-element.18), channel_id=1, source_target_pairs={{0,1},{1,2},{2,3},{3,4},{4,5},{5,6},{6,7},{7,8},{8,9},{9,10},{10,1... | collective-permute-start | bytes 245768 | tf_op jit(solution)/shard_map/ppermute | solution.py:337
  56.9 11.2 %collective-permute-start.6 = (bf16[48,512]{1,0:T(8,128)(2,1)S(1)}, bf16[48,512]{1,0:T(8,128)(2,1)S(1)}, u32[]{:S(2)}, u32[]{:S(2)}) collective-permute-start(bf16[48,512]{1,0:T(8,128)(2,1)S(1)} %add_convert_fusion.3), channel_id=1, source_target_pairs={{0,12},{1,13},{2,14},{3,15},{4,8},{5,9},{6,10},{7,11},{8,4},{9,5},... | collective-permute-start | bytes 147464 | tf_op jit(solution)/shard_map/ppermute | solution.py:341
  59.9 8.7 %collective-permute-start.5 = (bf16[48,512]{1,0:T(8,128)(2,1)S(1)}, bf16[48,512]{1,0:T(8,128)(2,1)S(1)}, u32[]{:S(2)}, u32[]{:S(2)}) collective-permute-start(bf16[48,512]{1,0:T(8,128)(2,1)S(1)} %add_convert_fusion.3), channel_id=1, source_target_pairs={{0,8},{1,9},{2,10},{3,11},{4,12},{5,13},{6,14},{7,15},{8,0},{9,1},... | collective-permute-start | bytes 147464 | tf_op jit(solution)/shard_map/ppermute | solution.py:341
  61.1 7.5 %collective-permute-start.4 = (bf16[48,512]{1,0:T(8,128)(2,1)S(1)}, bf16[48,512]{1,0:T(8,128)(2,1)S(1)}, u32[]{:S(2)}, u32[]{:S(2)}) collective-permute-start(bf16[48,512]{1,0:T(8,128)(2,1)S(1)} %add_convert_fusion.3), channel_id=1, source_target_pairs={{0,4},{1,5},{2,6},{3,7},{4,0},{5,1},{6,2},{7,3},{8,12},{9,13},{10,... | collective-permute-start | bytes 147464 | tf_op jit(solution)/shard_map/ppermute | solution.py:341
  68.6 12.1 %collective-permute-start.8 = (bf16[64,512]{1,0:T(8,128)(2,1)S(1)}, bf16[64,512]{1,0:T(8,128)(2,1)S(1)}, u32[]{:S(2)}, u32[]{:S(2)}) collective-permute-start(bf16[64,512]{1,0:T(8,128)(2,1)S(1)} %own_step.2.refs_0_), channel_id=1, source_target_pairs={{1,0},{2,1},{3,2},{4,3},{5,4},{6,5},{7,6},{8,7},{9,8},{10,9},{11,1... | collective-permute-start | bytes 196616 | tf_op jit(solution)/shard_map/ppermute | solution.py:337
  76.6 4.2 %collective-permute-start.9 = (bf16[48,512]{1,0:T(8,128)(2,1)S(1)}, bf16[48,512]{1,0:T(8,128)(2,1)S(1)}, u32[]{:S(2)}, u32[]{:S(2)}) collective-permute-start(bf16[48,512]{1,0:T(8,128)(2,1)S(1)} %add_convert_fusion.2.refs_2_), channel_id=1, source_target_pairs={{0,16},{1,17},{2,18},{3,19},{4,20},{5,21},{6,22},{7,23},{8,24},{9,... | collective-permute-start | bytes 147464 | tf_op jit(solution)/shard_map/ppermute | solution.py:341
  80.8 19.1 %copy-start.4 = (bf16[512,512]{1,0:T(8,128)(2,1)S(1)}, bf16[512,512]{1,0:T(8,128)(2,1)}, u32[]{:S(2)}) copy-start(bf16[512,512]{1,0:T(8,128)(2,1)} %constant.22.clone.m2) | copy-start | bytes 1572868
  125.4 11.6 %collective-permute-start.12 = (bf16[48,512]{1,0:T(8,128)(2,1)S(1)}, bf16[48,512]{1,0:T(8,128)(2,1)S(1)}, u32[]{:S(2)}, u32[]{:S(2)}) collective-permute-start(bf16[48,512]{1,0:T(8,128)(2,1)S(1)} %get-tuple-element.26), channel_id=1, source_target_pairs={{0,3},{1,2},{2,1},{3,0},{4,7},{5,6},{6,5},{7,4},{8,11},{9,10},{10,... | collective-permute-start | bytes 147464 | tf_op jit(solution)/shard_map/ppermute | solution.py:341
  134.5 4.1 %collective-permute-start.11 = (bf16[48,512]{1,0:T(8,128)(2,1)S(1)}, bf16[48,512]{1,0:T(8,128)(2,1)S(1)}, u32[]{:S(2)}, u32[]{:S(2)}) collective-permute-start(bf16[48,512]{1,0:T(8,128)(2,1)S(1)} %get-tuple-element.26), channel_id=1, source_target_pairs={{0,2},{1,3},{2,0},{3,1},{4,6},{5,7},{6,4},{7,5},{8,10},{9,11},{10,... | collective-permute-start | bytes 147464 | tf_op jit(solution)/shard_map/ppermute | solution.py:341
  134.5 4.1 %collective-permute-start.10 = (bf16[48,512]{1,0:T(8,128)(2,1)S(1)}, bf16[48,512]{1,0:T(8,128)(2,1)S(1)}, u32[]{:S(2)}, u32[]{:S(2)}) collective-permute-start(bf16[48,512]{1,0:T(8,128)(2,1)S(1)} %get-tuple-element.26), channel_id=1, source_target_pairs={{0,1},{1,0},{2,3},{3,2},{4,5},{5,4},{6,7},{7,6},{8,9},{9,8},{10,11... | collective-permute-start | bytes 147464 | tf_op jit(solution)/shard_map/ppermute | solution.py:341
  134.8 10.5 %collective-permute-start.16 = (bf16[64,512]{1,0:T(8,128)(2,1)S(1)}, bf16[64,512]{1,0:T(8,128)(2,1)S(1)}, u32[]{:S(2)}, u32[]{:S(2)}) collective-permute-start(bf16[64,512]{1,0:T(8,128)(2,1)S(1)} %get-tuple-element.28), channel_id=1, source_target_pairs={{0,1},{1,2},{2,3},{3,4},{4,5},{5,6},{6,7},{7,8},{8,9},{9,10},{10,1... | collective-permute-start | bytes 196616 | tf_op jit(solution)/shard_map/ppermute | solution.py:337
  138.7 10.1 %collective-permute-start.15 = (bf16[48,512]{1,0:T(8,128)(2,1)S(1)}, bf16[48,512]{1,0:T(8,128)(2,1)S(1)}, u32[]{:S(2)}, u32[]{:S(2)}) collective-permute-start(bf16[48,512]{1,0:T(8,128)(2,1)S(1)} %add_convert_fusion.1), channel_id=1, source_target_pairs={{0,12},{1,13},{2,14},{3,15},{4,8},{5,9},{6,10},{7,11},{8,4},{9,5},... | collective-permute-start | bytes 147464 | tf_op jit(solution)/shard_map/ppermute | solution.py:341
  138.8 10.0 %collective-permute-start.14 = (bf16[48,512]{1,0:T(8,128)(2,1)S(1)}, bf16[48,512]{1,0:T(8,128)(2,1)S(1)}, u32[]{:S(2)}, u32[]{:S(2)}) collective-permute-start(bf16[48,512]{1,0:T(8,128)(2,1)S(1)} %add_convert_fusion.1), channel_id=1, source_target_pairs={{0,8},{1,9},{2,10},{3,11},{4,12},{5,13},{6,14},{7,15},{8,0},{9,1},... | collective-permute-start | bytes 147464 | tf_op jit(solution)/shard_map/ppermute | solution.py:341
  138.9 10.7 %collective-permute-start.13 = (bf16[48,512]{1,0:T(8,128)(2,1)S(1)}, bf16[48,512]{1,0:T(8,128)(2,1)S(1)}, u32[]{:S(2)}, u32[]{:S(2)}) collective-permute-start(bf16[48,512]{1,0:T(8,128)(2,1)S(1)} %add_convert_fusion.1), channel_id=1, source_target_pairs={{0,4},{1,5},{2,6},{3,7},{4,0},{5,1},{6,2},{7,3},{8,12},{9,13},{10,... | collective-permute-start | bytes 147464 | tf_op jit(solution)/shard_map/ppermute | solution.py:341
  149.6 5.5 %collective-permute-start.17 = (bf16[48,512]{1,0:T(8,128)(2,1)S(1)}, bf16[48,512]{1,0:T(8,128)(2,1)S(1)}, u32[]{:S(2)}, u32[]{:S(2)}) collective-permute-start(bf16[48,512]{1,0:T(8,128)(2,1)S(1)} %add_convert_fusion.refs_1_), channel_id=1, source_target_pairs={{0,16},{1,17},{2,18},{3,19},{4,20},{5,21},{6,22},{7,23},{8,24},{9,... | collective-permute-start | bytes 147464 | tf_op jit(solution)/shard_map/ppermute | solution.py:341
